TPU v7x, 512 devices: a whole 4x8x8 slice. The times are simulated.
512 devices in a mesh: samp: 32 (over z, x_hi, core), box: 2 (over x_lo), rhs: 8 (over y).
Axes of the slice: x: 4 (x_hi: 2, x_lo: 2; x = x_hi * 2 + x_lo), y: 8, z: 8, core: 2. Of those that a mesh axis runs over, the one named last changes fastest.
Arguments:
- radiated: float32 [256, 16, 2, 4096], P(('box', 'samp'), 'rhs'), may hold values from -6 to 6
- low_table: float32 [320, 2, 4096], P(('box', 'rhs'), None, 'samp'), may hold values from -1.2 to 1.2
- high_table: float32 [320, 2, 16384], P(('box', 'rhs'), None, 'samp'), may hold values from -1.2 to 1.2
- low_sources: int32 [256, 16], P('box'), may hold values from 0 to 255
- low_operators: int32 [256, 16], P('box'), may hold values from 0 to 319
- high_sources: int32 [32, 16], P('box'), may hold values from 0 to 31
- high_operators: int32 [32, 16], P('box'), may hold values from 0 to 319
- stencil_index: int32 [16, 16384], replicated, may hold values from 0 to 4095, as said below
- stencil_weight: float32 [16, 16384], replicated, may hold values from -0.75 to 0.75
- shift_angle: float32 [8, 16384], replicated, may hold values from -3.140625 to 3.140625
Outputs:
- low_incoming: float32 [256, 16, 2, 4096], P('box', 'rhs', None, 'samp')
- high_incoming: float32 [32, 16, 2, 16384], P('box', 'rhs', None, 'samp')
Inputs may be any that keep to these rules, and one draw needn't show every extreme that they name: stencil_index[p, j] = min(max(j // 4 + o, 0), 4095) with an offset o of -32 to 32; for every j the offset at p = 0 is -32 and at p = 15 is 32.
All inputs are finite; a program needn't handle non-finite values.
Results may differ from a plain program's by a relative error of at most 0.000071.
Values sent between devices are 32-bit elements; how exact they have to be, the bound alone decides.
No kernel may reach another device: no remote copies, remote signals or barrier semaphores. Data moves between devices by JAX's collectives and lax.ppermute only.
A program may use at most 128 MiB of HBM per device.

v0:
```python
import jax
import jax.numpy as jnp
from jax import lax
from jax.experimental import pallas as pl
from jax.experimental.pallas import tpu as pltpu
from jax.sharding import PartitionSpec as P

F32, BF16, I32 = jnp.float32, jnp.bfloat16, jnp.int32
VMEM = pl.BlockSpec(memory_space=pltpu.VMEM)
SMEM = pl.BlockSpec(memory_space=pltpu.SMEM)
HBM = pl.BlockSpec(memory_space=pltpu.HBM)
LANES = 128
ROWS = 120
ALL_VMEM = 63 << 20
SENT = ROWS + 16


def call(kernel, ins, outs, scratch=(), flops=0, moved=0, out_place=VMEM, room=24 << 20):
    return pl.pallas_call(
        kernel,
        in_specs=list(ins),
        out_specs=[out_place] * len(outs),
        out_shape=[jax.ShapeDtypeStruct(s, d) for s, d in outs],
        scratch_shapes=list(scratch),
        compiler_params=pltpu.CompilerParams(vmem_limit_bytes=room),
        cost_estimate=pl.CostEstimate(flops=flops, bytes_accessed=moved, transcendentals=0),
    )


def halves(x):
    high = x.astype(BF16)
    return high, (x - high.astype(F32)).astype(BF16)


def row_of(shape=(8, LANES)):
    return lax.broadcasted_iota(I32, shape, 0)


def lane_of(shape=(8, LANES)):
    return lax.broadcasted_iota(I32, shape, 1)


def run_all(copies):
    for copy in copies:
        copy.start()
    for copy in copies:
        copy.wait()


def repeat(count, step, body):
    def several(n, carry):
        for i in range(step):
            body(n * step + i)
        return carry

    lax.fori_loop(0, count // step, several, 0)


def across(x, row):
    return jnp.broadcast_to(x[row : row + 1, :], (8, LANES))


def product3(left, right, dims):
    (lh, ll), (rh, rl) = left, right
    dot = lambda a, b: lax.dot_general(a, b, (dims, ((), ())), preferred_element_type=F32)
    return dot(lh, rh) + (dot(lh, rl) + dot(ll, rh))


def table_kernel(
    low_hbm, high_hbm, sources_hbm, operators_hbm, keep, give, low, high, sources, operators, sem
):
    half = lax.axis_index("box")
    run_all(
        [
            pltpu.make_async_copy(low_hbm, low, sem.at[0]),
            pltpu.make_async_copy(high_hbm, high, sem.at[1]),
            pltpu.make_async_copy(sources_hbm, sources, sem.at[2]),
            pltpu.make_async_copy(operators_hbm, operators, sem.at[3]),
        ]
    )
    for out, b in ((keep, half), (give, 1 - half)):
        for op in range(20):
            for jh in range(2):
                lanes = pl.ds(pl.multiple_of((2 * b + jh) * LANES, LANES), LANES)
                at = 4 * op + 2 * jh
                out[at : at + 2, :] = high[op, :, lanes]
            out[80 + 2 * op : 82 + 2 * op, :] = low[op]
    give[ROWS:, :] = jnp.zeros((16, LANES), F32)
    give[ROWS:, 0:16] = sources[...].astype(F32)
    give[ROWS:, 16:32] = operators[...].astype(F32)


def ready_kernel(
    rad_hbm, index, weight, angle,
    win_out, wh_out, wl_out, mh_out, ml_out, ci_out, si_out, cx_out, sx_out,
    rad, rows, win, idx, wgt, ang, wh, wl, mh, ml, ci, si, cx, sx, sem, out_sem,
):
    seg, half = lax.axis_index("samp"), lax.axis_index("box")
    start = pl.multiple_of(seg * 512, LANES)
    total = index.shape[1]
    before = pl.multiple_of(jnp.maximum(start - LANES, 0), LANES)
    after = pl.multiple_of(jnp.minimum(start + 512, total - LANES), LANES)
    first = pltpu.make_async_copy(rad_hbm, rad, sem.at[9])
    first.start()
    copies = []
    for n, (src, dst) in enumerate(((index, idx), (weight, wgt), (angle, ang))):
        for m, (at, to, width) in enumerate(((before, 0, 128), (start, 128, 512), (after, 640, 128))):
            copies.append(
                pltpu.make_async_copy(
                    src.at[:, pl.ds(at, width)], dst.at[:, to : to + width], sem.at[3 * n + m]
                )
            )
    for copy in copies:
        copy.start()
    first.wait()
    for c in range(2):
        for o in range(4):
            for r in range(2):
                row = c * 8 + (o // 2) * 4 + r * 2 + o % 2
                rows[row : row + 1, :] = rad[o, r, c : c + 1, :]
    n_samp = rows.shape[1] // LANES
    lane = lane_of((16, LANES))
    lane8 = lane_of()
    block = lambda s: rows[:, (s % n_samp) * LANES : (s % n_samp + 1) * LANES]
    for s in range(n_samp):
        here = block(s)
        real, imag = here[:8], pltpu.roll(here[8:], 64, 1)
        for b, near, low, rest in ((0, s - 1, 0, 96), (1, s + 1, 32, 128)):
            inside = (lane >= low) & (lane < rest)
            inside8 = (lane8 >= low) & (lane8 < rest)
            win[b * n_samp + s, :16, :] = jnp.where(inside, here, block(near))
            win[b * n_samp + s, 16:, :] = jnp.where(inside8, imag, real)
    last = [pltpu.make_async_copy(win, win_out, out_sem.at[0])]
    last[0].start()
    for copy in copies:
        copy.wait()
    slot = lax.broadcasted_iota(I32, (LANES, LANES), 0)

    def band(at, first):
        at = pl.multiple_of(at, LANES)
        found = idx[:, pl.ds(at, LANES)]
        found = found & 127 if first is None else found - first
        value = wgt[:, pl.ds(at, LANES)]
        matrix = jnp.zeros((LANES, LANES), F32)
        for p in range(16):
            matrix += jnp.where(found[p : p + 1, :] == slot, value[p : p + 1, :], 0.0)
        return halves(matrix)

    own = pl.multiple_of(LANES + 256 * half, LANES)

    def interp(n):
        at = pl.multiple_of(n * LANES, LANES)
        wh[:, pl.ds(at, LANES)], wl[:, pl.ds(at, LANES)] = band(own + at, None)

    def anterp(n):
        at = pl.multiple_of(n * LANES, LANES)
        mh[:, pl.ds(at, LANES)], ml[:, pl.ds(at, LANES)] = band(at, seg * 128)

    repeat(2, 2, interp)
    repeat(6, 2, anterp)
    cosine, sine = jnp.cos(ang[...]), jnp.sin(ang[...])
    spin = jnp.where(row_of((4, 768)) % 2 == 0, 1.0, -1.0)
    cx[...] = jnp.concatenate([jnp.broadcast_to(cosine[o : o + 1], (4, 768)) for o in range(8)], 0)
    sx[...] = jnp.concatenate(
        [jnp.broadcast_to(sine[o : o + 1], (4, 768)) * spin for o in range(8)], 0
    )
    for out, x in ((ci, cosine), (si, sine)):
        ang[...] = x
        mine = ang[:, pl.ds(own, 256)]
        for h in range(2):
            pair = [mine[4 * h + 2 * q : 4 * h + 2 * q + 2] for q in range(2)]
            out[h] = jnp.concatenate([pair[0], pair[0], pair[1], pair[1]], 0)
    made = ((wh, wh_out), (wl, wl_out), (mh, mh_out), (ml, ml_out))
    made += ((ci, ci_out), (si, si_out), (cx, cx_out), (sx, sx_out))
    for n, (src, dst) in enumerate(made):
        last.append(pltpu.make_async_copy(src, dst, out_sem.at[n + 1]))
        last[-1].start()
    for copy in last:
        copy.wait()


def upper_kernel(
    tab, got, sources, operators, win, wh_in, wl_in, ci_in, si_in,
    own, oth, rim_own, rim_oth,
    tre, tim, full, pat, pat_sw, wh, wl, ci, si, lists, scalars, sem,
):
    copies = [
        pltpu.make_async_copy(src, dst, sem.at[n])
        for n, (src, dst) in enumerate(((wh_in, wh), (wl_in, wl), (ci_in, ci), (si_in, si)))
    ]
    for copy in copies:
        copy.start()
    lists[:16, 0:16] = sources[...] * 8
    lists[:16, 16:32] = operators[...] * 8
    lists[16:, :] = (got[ROWS:, :] * 8.0).astype(I32)
    listed = pltpu.make_async_copy(lists, scalars, sem.at[4])
    listed.start()
    row = row_of()
    upper, even = row < 4, row % 2 == 0
    flip = jnp.where(even, -1.0, 1.0)
    half = lax.axis_index("box")

    def device(n):
        q = n % 2
        first = (lax.bitwise_xor(q, half) * 8 + n // 2) * 160
        for i in range(20):
            four = tab[n // 2, q, 4 * i : 4 * i + 4, :]
            at = pl.multiple_of(first + 8 * i, 8)
            tre[pl.ds(at, 8), :] = jnp.where(upper, across(four, 0), across(four, 2))
            tim[pl.ds(at, 8), :] = jnp.where(upper, across(four, 1), across(four, 3)) * flip

    repeat(16, 2, device)
    for copy in copies:
        copy.wait()

    def interpolate(n):
        at = pl.multiple_of(n * 128, 128)
        rows = jnp.concatenate([win[n * 8 + q, :16, :] for q in range(8)], 0)
        full[pl.ds(at, 128), :] = product3(
            halves(rows), (wh[...], wl[...]), ((1,), (0,))
        )

    repeat(8, 4, interpolate)

    def aggregate(n):
        u = n
        at = pl.multiple_of(u * 32, 32)
        er, ei, gr, gi = (full[pl.ds(at + 8 * q, 8), :] for q in range(4))
        c0, s0, c1, s1 = ci[0], si[0], ci[1], si[1]
        real = c0 * er - s0 * ei + (c1 * gr - s1 * gi)
        imag = c0 * ei + s0 * er + (c1 * gi + s1 * gr)
        lay, lay_sw = [], []
        for h in range(2):
            re, im = real[:, h * LANES : (h + 1) * LANES], imag[:, h * LANES : (h + 1) * LANES]
            re, im = re + pltpu.roll(re, 4, 0), im + pltpu.roll(im, 4, 0)
            re, im = re + pltpu.roll(re, 7, 0), im + pltpu.roll(im, 7, 0)
            lay.append(jnp.where(even, re, pltpu.roll(im, 1, 0)))
            lay_sw.append(jnp.where(even, im, pltpu.roll(re, 1, 0)))
        to = pl.ds(pl.multiple_of(u * 8, 8), 8)
        pat[to, :] = jnp.where(upper, lay[0], lay[1])
        pat_sw[to, :] = jnp.where(upper, lay_sw[0], lay_sw[1])

    repeat(32, 4, aggregate)

    listed.wait()

    def target(u):
        acc = jnp.zeros((8, LANES), F32)
        acc2 = jnp.zeros((8, LANES), F32)
        for e in range(16):
            src = pl.ds(pl.multiple_of(scalars[u, e], 8), 8)
            op = pl.ds(pl.multiple_of(scalars[u, 16 + e], 8), 8)
            acc += tre[op, :] * pat[src, :]
            acc2 += tim[op, :] * pat_sw[src, :]
        return acc + acc2

    def translate(shift, whole, rim):
        def pair(n):
            one, two = target(2 * n + shift), target(2 * n + 1 + shift)
            whole[2 * n], whole[2 * n + 1] = one, two
            first = jnp.where(upper, one, pltpu.roll(two, 4, 0))
            last = jnp.where(upper, pltpu.roll(one, 4, 0), two)
            rim[n] = jnp.where(half == 0, first, last)

        repeat(8, 2, pair)

    translate(0, own, rim_own)
    translate(16, oth, rim_oth)


def lower_kernel(sources, operators, win, tab, out, t8, pat, lists, scalars, sem):
    lists[:16, :] = sources[...] * 8
    lists[16:, :] = operators[...] * 8
    listed = pltpu.make_async_copy(lists, scalars, sem)
    listed.start()
    row, lane = row_of(), lane_of()
    half = lax.axis_index("box")
    upper, lane_half = row < 4, half * 96
    flip = jnp.where(row % 2 == 0, -1.0, 1.0)

    def device(n):
        q = n % 2
        first = (lax.bitwise_xor(q, half) * 8 + n // 2) * 160
        for i in range(20):
            two = tab[n // 2, q, 80 + 2 * i : 82 + 2 * i, :]
            at = pl.multiple_of(first + 8 * i, 8)
            t8[pl.ds(at, 8), :] = jnp.where(upper, across(two, 0), across(two, 1) * flip)

    repeat(16, 2, device)
    absent = (lane >= 96 - lane_half) & (lane < 128 - lane_half)
    kinds = [(row == 0) | (row == 2), (row == 1) | (row == 3), (row == 4) | (row == 6)]

    def spread_out(n):
        extra = win[n, 16:24, :]
        real = jnp.where(absent, extra, win[n, 0:8, :])
        imag = jnp.where(absent, pltpu.roll(extra, 64, 1), win[n, 8:16, :])
        real_t, imag_t = pltpu.roll(real, 4, 0), pltpu.roll(imag, 4, 0)
        for o2 in range(2):
            if o2 == 0:
                re, im = jnp.where(upper, real, real_t), jnp.where(upper, imag, imag_t)
            else:
                re, im = jnp.where(upper, real_t, real), jnp.where(upper, imag_t, imag)
            later = [re, pltpu.roll(im, 1, 0), im, pltpu.roll(re, 1, 0)]
            sooner = [pltpu.roll(re, 7, 0), im, pltpu.roll(im, 7, 0), re]
            for o, (a, b, c, d) in enumerate((later, sooner)):
                at = pl.multiple_of(n * 32 + 8 * (2 * o2 + o), 8)
                pat[pl.ds(at, 8), :] = jnp.where(
                    kinds[0], a, jnp.where(kinds[1], b, jnp.where(kinds[2], c, d))
                )

    repeat(64, 8, spread_out)
    listed.wait()

    def four(n):
        sums = []
        for q in range(4):
            t = n * 4 + q
            acc = [jnp.zeros((8, LANES), F32)] * 2
            for e in range(16):
                op = pl.ds(pl.multiple_of(scalars[16 + e, t], 8), 8)
                src = pl.ds(pl.multiple_of(scalars[e, t], 8), 8)
                acc[e % 2] += t8[op, :] * pat[src, :]
            total = acc[0] + acc[1]
            sums.append(total + pltpu.roll(total, 4, 0))
        out[2 * n] = jnp.where(upper, sums[0], sums[1])
        out[2 * n + 1] = jnp.where(upper, sums[2], sums[3])

    repeat(32, 1, four)


def final_kernel(
    own, got, rim_a, rim_b, low, mh, ml, cx, sx, low_out, high_out, lh, ll
):
    row = row_of()
    upper, even = row < 4, row % 2 == 0
    first = lax.axis_index("box") == 0

    def swap(x):
        return jnp.where(even, pltpu.roll(x, 7, 0), pltpu.roll(x, 1, 0))

    def pair(n):
        rims = (jnp.where(first, rim_b[n], rim_a[n]), jnp.where(first, rim_a[n], rim_b[n]))
        for q in range(2):
            u = 2 * n + q
            one = jnp.where(first, own[u], got[u])
            two = jnp.where(first, got[u], own[u])
            for jt, x in enumerate((one, one, two, two)):
                for r in range(2):
                    high_out[u, r, :, jt * LANES : (jt + 1) * LANES] = x[
                        4 * (jt % 2) + 2 * r : 4 * (jt % 2) + 2 * r + 2, :
                    ]
            blocks = []
            for x in (one, two):
                turned = pltpu.roll(x, 4, 0)
                blocks += [jnp.where(upper, x, turned), jnp.where(upper, turned, x)]
            edge = []
            for x in rims:
                turned = pltpu.roll(x, 4, 0)
                edge.append(jnp.where(upper, x, turned) if q == 0 else jnp.where(upper, turned, x))
            blocks = [edge[0]] + blocks + [edge[1]]
            at = pl.multiple_of(u * 32, 32)
            for jt, x in enumerate(blocks):
                lanes = slice(jt * LANES, (jt + 1) * LANES)
                y = swap(x)
                rows = jnp.concatenate(
                    [
                        cx[8 * g : 8 * g + 8, lanes] * x + sx[8 * g : 8 * g + 8, lanes] * y
                        for g in range(4)
                    ],
                    0,
                )
                lh[pl.ds(at, 32), lanes], ll[pl.ds(at, 32), lanes] = halves(rows)

    repeat(8, 2, pair)

    def block(n):
        at = pl.multiple_of(n * 128, 128)
        sums = product3(
            (lh[pl.ds(at, 128), :], ll[pl.ds(at, 128), :]), (mh[...], ml[...]), ((1,), (1,))
        )
        low_out[pl.ds(at, 128), :] = sums + low[pl.ds(at, 128), :]

    repeat(4, 2, block)


def shards(
    radiated,
    low_table,
    high_table,
    low_sources,
    low_operators,
    high_sources,
    high_operators,
    stencil_index,
    stencil_weight,
    shift_angle,
):
    n_samp = lax.axis_size("samp")
    dma = pltpu.SemaphoreType.DMA
    keep, give = call(
        table_kernel,
        [HBM] * 4,
        [((ROWS, LANES), F32), ((SENT, LANES), F32)],
        [pltpu.VMEM((20, 2, LANES), F32), pltpu.VMEM((20, 2, 512), F32)]
        + [pltpu.VMEM((16, 16), I32)] * 2
        + [dma((4,))],
        moved=1 << 20,
        room=ALL_VMEM,
    )(low_table, high_table, high_sources, high_operators)
    got = lax.ppermute(give, "box", [(0, 1), (1, 0)])
    made = [
        ((64, 24, LANES), F32),
        ((LANES, 256), BF16),
        ((LANES, 256), BF16),
        ((LANES, 768), BF16),
        ((LANES, 768), BF16),
        ((2, 8, 256), F32),
        ((2, 8, 256), F32),
        ((32, 768), F32),
        ((32, 768), F32),
    ]
    win, wh, wl, mh, ml, ci, si, cx, sx = call(
        ready_kernel,
        [HBM] * 4,
        made,
        [pltpu.VMEM((4, 2, 2, 4096), F32), pltpu.VMEM((16, 4096), F32), pltpu.VMEM(*made[0])]
        + [pltpu.VMEM((16, 768), I32), pltpu.VMEM((16, 768), F32), pltpu.VMEM((8, 768), F32)]
        + [pltpu.VMEM(*x) for x in made[1:]]
        + [dma((10,)), dma((9,))],
        flops=10 << 20,
        moved=8 << 20,
        out_place=HBM,
        room=ALL_VMEM,
    )(radiated, stencil_index, stencil_weight, shift_angle)
    win, got = lax.optimization_barrier((win, got))
    win = lax.all_to_all(win, ("box", "samp"), 0, 0, tiled=True)
    tab = lax.all_gather(jnp.stack([keep, got[:ROWS]]), "rhs")
    part, rim = ((16, 8, LANES), F32), ((8, 8, LANES), F32)
    own, oth, rim_own, rim_oth = call(
        upper_kernel,
        [VMEM] * 5 + [HBM] * 4,
        [part, part, rim, rim],
        [
            pltpu.VMEM((2560, LANES), F32),
            pltpu.VMEM((2560, LANES), F32),
            pltpu.VMEM((1024, 256), F32),
            pltpu.VMEM((256, LANES), F32),
            pltpu.VMEM((256, LANES), F32),
            pltpu.VMEM(*made[1]),
            pltpu.VMEM(*made[2]),
            pltpu.VMEM(*made[5]),
            pltpu.VMEM(*made[6]),
            pltpu.VMEM((32, LANES), I32),
            pltpu.SMEM((32, LANES), I32),
            dma((5,)),
        ],
        flops=200 << 20,
        moved=6 << 20,
    )(tab, got, high_sources, high_operators, win, wh, wl, ci, si)
    flat = lambda s, b: 2 * s + b
    other = lax.ppermute(oth, "box", [(0, 1), (1, 0)])
    down = [(flat(s, 0), s - 1) for s in range(1, n_samp)]
    up = [(flat(s, 1), s + 1) for s in range(n_samp - 1)]
    both = ("samp", "box")
    rim_a = lax.ppermute(
        rim_own, both, [(i, flat(s, 0)) for i, s in down] + [(i, flat(s, 1)) for i, s in up]
    )
    rim_b = lax.ppermute(
        rim_oth, both, [(i, flat(s, 1)) for i, s in down] + [(i, flat(s, 0)) for i, s in up]
    )
    (low,) = call(
        lower_kernel,
        [VMEM] * 4,
        [((64, 8, LANES), F32)],
        [
            pltpu.VMEM((2560, LANES), F32),
            pltpu.VMEM((2048, LANES), F32),
            pltpu.VMEM((32, LANES), I32),
            pltpu.SMEM((32, LANES), I32),
            dma,
        ],
        flops=20 << 20,
        moved=10 << 20,
    )(low_sources.T, low_operators.T, win, tab)
    low_incoming, high_incoming = call(
        final_kernel,
        [VMEM] * 9,
        [((512, LANES), F32), ((16, 2, 2, 512), F32)],
        [pltpu.VMEM((512, 768), BF16), pltpu.VMEM((512, 768), BF16)],
        flops=300 << 20,
        moved=4 << 20,
    )(own, other, rim_a, rim_b, low.reshape(512, LANES), mh, ml, cx, sx)
    return low_incoming.reshape(128, 2, 2, LANES), high_incoming


def solution(mesh):
    return jax.shard_map(
        shards,
        mesh=mesh,
        in_specs=(
            P(("box", "samp"), "rhs", None, None),
            P(("box", "rhs"), None, "samp"),
            P(("box", "rhs"), None, "samp"),
            P("box", None),
            P("box", None),
            P("box", None),
            P("box", None),
            P(),
            P(),
            P(),
        ),
        out_specs=(P("box", "rhs", None, "samp"), P("box", "rhs", None, "samp")),
        check_vma=False,
    )
```

profile of v0, /device:TPU:64, one launch (start us, length us, event | category | flops | bytes accessed | tf_op | source)
XLA Modules:
  0.0 74.9 jit_solution(12252018445943867071)
XLA Ops:
  0.6 1.6 %shard_map.113 = (f32[120,128]{1,0:T(8,128)}, f32[136,128]{1,0:T(8,128)}) custom-call(f32[20,2,128]{2,1,0:T(2,128)} %low_hbm.1, f32[20,2,512]{2,1,0:T(2,128)} %high_hbm.1, s32[16,16]{1,0:T(8,128)} %sources.1, s32[16,16]{1,0:T(8,128)} %operators.1), custom_call_target="tpu_custom_call" | custom-call | bytes 1048576 | tf_op jit(solution)/shard_map/pallas_call | solution.py:400
  2.3 3.4 %collective-permute-start = (f32[136,128]{1,0:T(8,128)}, f32[136,128]{1,0:T(8,128)S(1)}, u32[]{:S(2)}, u32[]{:S(2)}) collective-permute-start(f32[136,128]{1,0:T(8,128)} %get-tuple-element.23), channel_id=1, source_target_pairs={{0,8},{8,0},{1,9},{9,1},{2,10},{10,2},{3,11},{11,3},{4,12},{12,4},... | collective-permute-start | bytes 208904 | tf_op jit(solution)/shard_map/ppermute | solution.py:410
  5.7 3.2 %shard_map.114 = (f32[64,24,128]{2,1,0:T(8,128)}, bf16[128,256]{1,0:T(8,128)(2,1)}, bf16[128,256]{1,0:T(8,128)(2,1)}, bf16[128,768]{1,0:T(8,128)(2,1)}, bf16[128...) custom-call(f32[4,2,2,4096]{3,2,1,0:T(2,128)} %rad_hbm.1, ...), custom_call_target="tpu_custom_call" | custom-call | flops 10485760 | bytes 8388608 | tf_op jit(solution)/shard_map/pallas_call | solution.py:422
  8.9 0.0 collective-permute-done.got
  9.0 12.7 %all-to-all-start = ((f32[64,24,128]{2,1,0:T(8,128)}), f32[64,24,128]{2,1,0:T(8,128)S(1)}, u32[]{:S(2)}, u32[]{:S(2)}) async-start(f32[64,24,128]{2,1,0:T(8,128)} %get-tuple-element.25), calls=%async_computation | async-start | bytes 1572864 | tf_op jit(solution)/shard_map/all_to_all | solution.py:436
  21.7 0.0 copy-start.12
  21.7 0.8 %copy-done.12 = f32[120,128]{1,0:T(8,128)S(1)} copy-done((f32[120,128]{1,0:T(8,128)S(1)}, f32[120,128]{1,0:T(8,128)}, u32[]{:S(2)}) %copy-start.12) | copy-done | bytes 61464
  22.5 0.0 copy-start.1
  22.6 0.0 copy-start.3
  22.6 0.0 copy-start.4
  22.6 0.0 copy-start.5
  22.6 28.3 %all-gather = f32[16,120,128]{2,1,0:T(8,128)S(1)} all-gather(f32[2,120,128]{2,1,0:T(8,128)S(1)} %pad_maximum_fusion), channel_id=2, replica_groups=mesh['samp'=32,'box'=2,'rhs'=8] {'rhs'}, dimensions={0}, use_global_device_ids=true | all-gather | bytes 1105920 | tf_op jit(solution)/shard_map/all_gather | solution.py:437
  50.9 0.0 all-to-all-done.win
  50.9 0.0 copy-done
  50.9 0.0 copy-done.1
  50.9 0.0 copy-done.3
  50.9 0.0 copy-done.4
  50.9 0.0 copy-done.5
  50.9 0.6 copy-done.2
  51.6 2.9 %shard_map.115 = (f32[16,8,128]{2,1,0:T(8,128)S(1)}, f32[16,8,128]{2,1,0:T(8,128)S(1)}, f32[8,8,128]{2,1,0:T(8,128)S(1)}, f32[8,8,128]{2,1,0:T(8,128)S(1)}) custom-call(f32[8,2,120,128]{3,2,1,0:T(8,128)S(1)} %bitcast.8, f32[136,128]{1,0:T(8,128)S(1)} %collective-permute-done.got, s32[16,16]{1,0:T(8,128)S(1)} %copy-done.2, s32[16,16]{1,0:T(8,128)S(1)} %copy-done.3, ...), custom_call_target="tpu_custom_call" | custom-call | flops 209715200 | bytes 6291456 | tf_op jit(solution)/shard_map/pallas_call | solution.py:439
  54.5 0.0 copy-start.6
  54.5 3.5 %collective-permute-start.1 = (f32[16,8,128]{2,1,0:T(8,128)S(1)}, f32[16,8,128]{2,1,0:T(8,128)S(1)}, u32[]{:S(2)}, u32[]{:S(2)}) collective-permute-start(f32[16,8,128]{2,1,0:T(8,128)S(1)} %get-tuple-element.31), channel_id=1, source_target_pairs={{0,8},{8,0},{1,9},{9,1},{2,10},{10,2},{3,11},{11,3},{4,12},{12,4},... | collective-permute-start | bytes 196616 | tf_op jit(solution)/shard_map/ppermute | solution.py:461
  58.0 1.9 %collective-permute-start.2 = (f32[8,8,128]{2,1,0:T(8,128)S(1)}, f32[8,8,128]{2,1,0:T(8,128)S(1)}, u32[]{:S(2)}, u32[]{:S(2)}) collective-permute-start(f32[8,8,128]{2,1,0:T(8,128)S(1)} %get-tuple-element.32), channel_id=1, source_target_pairs={{16,0},{32,16},{48,32},{64,48},{80,64},{96,80},{112,96},{128,112},... | collective-permute-start | bytes 98312 | tf_op jit(solution)/shard_map/ppermute | solution.py:465
  60.0 5.6 %collective-permute-start.3 = (f32[8,8,128]{2,1,0:T(8,128)S(1)}, f32[8,8,128]{2,1,0:T(8,128)S(1)}, u32[]{:S(2)}, u32[]{:S(2)}) collective-permute-start(f32[8,8,128]{2,1,0:T(8,128)S(1)} %get-tuple-element.33), channel_id=1, source_target_pairs={{16,8},{32,24},{48,40},{64,56},{80,72},{96,88},{112,104},{128,120}... | collective-permute-start | bytes 98312 | tf_op jit(solution)/shard_map/ppermute | solution.py:468
  65.6 0.0 copy-start.8
  65.6 0.0 copy-start.10
  65.6 0.0 copy-start.11
  65.7 7.0 %shard_map.116 = f32[64,8,128]{2,1,0:T(8,128)S(1)} custom-call(s32[16,128]{1,0:T(8,128)S(1)} %bitcast.11, s32[16,128]{1,0:T(8,128)S(1)} %bitcast.12, f32[64,24,128]{2,1,0:T(8,128)S(1)} %all-to-all-done.win, f32[8,2,120,128]{3,2,1,0:T(8,128)S(1)} %bitcast.9), custom_call_target="tpu_custom_call" | custom-call | flops 20971520 | bytes 10485760 | tf_op jit(solution)/shard_map/pallas_call | solution.py:471
  72.6 0.0 collective-permute-done.2.rim_a
  72.6 0.0 collective-permute-done.3.rim_b
  72.6 0.0 collective-permute-done.1.got
  72.7 2.3 %shard_map.117 = (f32[512,128]{1,0:T(8,128)}, f32[16,2,2,512]{3,2,1,0:T(2,128)}) custom-call(f32[16,8,128]{2,1,0:T(8,128)S(1)} %get-tuple-element.30.own, f32[16,8,128]{2,1,0:T(8,128)S(1)} %collective-permute-done.1.got, f32[8,8,128]{2,1,0:T(8,128)S(1)} %collective-permute-done.2.rim_a, f32[8,8,128]{2,1,0:T(8,128)S(1)} %collective-permute-done.3.rim_b, ...), custom_call_target="tpu_custom_call" | custom-call | flops 314572800 | bytes 4194304 | tf_op jit(solution)/shard_map/pallas_call | solution.py:485
  (12 shorter events, 0.0 us)
Async XLA Ops:
  2.3 6.7 %collective-permute-start = (f32[136,128]{1,0:T(8,128)}, f32[136,128]{1,0:T(8,128)S(1)}, u32[]{:S(2)}, u32[]{:S(2)}) collective-permute-start(f32[136,128]{1,0:T(8,128)} %get-tuple-element.23), channel_id=1, source_target_pairs={{0,8},{8,0},{1,9},{9,1},{2,10},{10,2},{3,11},{11,3},{4,12},{12,4},... | collective-permute-start | bytes 208904 | tf_op jit(solution)/shard_map/ppermute | solution.py:410
  9.0 41.9 %all-to-all-start = ((f32[64,24,128]{2,1,0:T(8,128)}), f32[64,24,128]{2,1,0:T(8,128)S(1)}, u32[]{:S(2)}, u32[]{:S(2)}) async-start(f32[64,24,128]{2,1,0:T(8,128)} %get-tuple-element.25), calls=%async_computation | async-start | bytes 1572864 | tf_op jit(solution)/shard_map/all_to_all | solution.py:436
  21.7 0.8 %copy-start.12 = (f32[120,128]{1,0:T(8,128)S(1)}, f32[120,128]{1,0:T(8,128)}, u32[]{:S(2)}) copy-start(f32[120,128]{1,0:T(8,128)} %get-tuple-element.21) | copy-start | bytes 184324
  22.5 28.4 %copy-start = (bf16[128,256]{1,0:T(8,128)(2,1)S(1)}, bf16[128,256]{1,0:T(8,128)(2,1)}, u32[]{:S(2)}) copy-start(bf16[128,256]{1,0:T(8,128)(2,1)} %get-tuple-element.26.wh_in) | copy-start | bytes 196612
  22.5 28.4 %copy-start.1 = (bf16[128,256]{1,0:T(8,128)(2,1)S(1)}, bf16[128,256]{1,0:T(8,128)(2,1)}, u32[]{:S(2)}) copy-start(bf16[128,256]{1,0:T(8,128)(2,1)} %get-tuple-element.27.wl_in) | copy-start | bytes 196612
  22.6 28.4 %copy-start.3 = (s32[16,16]{1,0:T(8,128)S(1)}, s32[16,16]{1,0:T(8,128)}, u32[]{:S(2)}) copy-start(s32[16,16]{1,0:T(8,128)} %operators.1) | copy-start | bytes 3076
  22.6 28.4 %copy-start.4 = (f32[2,8,256]{2,1,0:T(8,128)S(1)}, f32[2,8,256]{2,1,0:T(8,128)}, u32[]{:S(2)}) copy-start(f32[2,8,256]{2,1,0:T(8,128)} %get-tuple-element.28.ci_in) | copy-start | bytes 49156
  22.6 28.4 %copy-start.5 = (f32[2,8,256]{2,1,0:T(8,128)S(1)}, f32[2,8,256]{2,1,0:T(8,128)}, u32[]{:S(2)}) copy-start(f32[2,8,256]{2,1,0:T(8,128)} %get-tuple-element.29.si_in) | copy-start | bytes 49156
  50.9 0.7 copy-start.2
  51.6 14.0 %copy-start.7 = (s32[128,16]{0,1:T(8,128)S(1)}, s32[128,16]{0,1:T(8,128)}, u32[]{:S(2)}) copy-start(s32[128,16]{0,1:T(8,128)} %param.14) | copy-start | bytes 24580
  54.5 11.1 %copy-start.6 = (s32[128,16]{0,1:T(8,128)S(1)}, s32[128,16]{0,1:T(8,128)}, u32[]{:S(2)}) copy-start(s32[128,16]{0,1:T(8,128)} %param.13) | copy-start | bytes 24580
  54.5 18.1 %collective-permute-start.1 = (f32[16,8,128]{2,1,0:T(8,128)S(1)}, f32[16,8,128]{2,1,0:T(8,128)S(1)}, u32[]{:S(2)}, u32[]{:S(2)}) collective-permute-start(f32[16,8,128]{2,1,0:T(8,128)S(1)} %get-tuple-element.31), channel_id=1, source_target_pairs={{0,8},{8,0},{1,9},{9,1},{2,10},{10,2},{3,11},{11,3},{4,12},{12,4},... | collective-permute-start | bytes 196616 | tf_op jit(solution)/shard_map/ppermute | solution.py:461
  58.0 14.6 %collective-permute-start.2 = (f32[8,8,128]{2,1,0:T(8,128)S(1)}, f32[8,8,128]{2,1,0:T(8,128)S(1)}, u32[]{:S(2)}, u32[]{:S(2)}) collective-permute-start(f32[8,8,128]{2,1,0:T(8,128)S(1)} %get-tuple-element.32), channel_id=1, source_target_pairs={{16,0},{32,16},{48,32},{64,48},{80,64},{96,80},{112,96},{128,112},... | collective-permute-start | bytes 98312 | tf_op jit(solution)/shard_map/ppermute | solution.py:465
  60.0 12.7 %collective-permute-start.3 = (f32[8,8,128]{2,1,0:T(8,128)S(1)}, f32[8,8,128]{2,1,0:T(8,128)S(1)}, u32[]{:S(2)}, u32[]{:S(2)}) collective-permute-start(f32[8,8,128]{2,1,0:T(8,128)S(1)} %get-tuple-element.33), channel_id=1, source_target_pairs={{16,8},{32,24},{48,40},{64,56},{80,72},{96,88},{112,104},{128,120}... | collective-permute-start | bytes 98312 | tf_op jit(solution)/shard_map/ppermute | solution.py:468
  65.6 7.0 %copy-start.8 = (bf16[128,768]{1,0:T(8,128)(2,1)S(1)}, bf16[128,768]{1,0:T(8,128)(2,1)}, u32[]{:S(2)}) copy-start(bf16[128,768]{1,0:T(8,128)(2,1)} %get-tuple-element.34.mh) | copy-start | bytes 589828
  65.6 7.0 %copy-start.9 = (bf16[128,768]{1,0:T(8,128)(2,1)S(1)}, bf16[128,768]{1,0:T(8,128)(2,1)}, u32[]{:S(2)}) copy-start(bf16[128,768]{1,0:T(8,128)(2,1)} %get-tuple-element.35.ml) | copy-start | bytes 589828
  65.6 7.0 %copy-start.10 = (f32[32,768]{1,0:T(8,128)S(1)}, f32[32,768]{1,0:T(8,128)}, u32[]{:S(2)}) copy-start(f32[32,768]{1,0:T(8,128)} %get-tuple-element.36.cx) | copy-start | bytes 294916
  65.6 7.0 %copy-start.11 = (f32[32,768]{1,0:T(8,128)S(1)}, f32[32,768]{1,0:T(8,128)}, u32[]{:S(2)}) copy-start(f32[32,768]{1,0:T(8,128)} %get-tuple-element.37.sx) | copy-start | bytes 294916
where the time goes:
time: 75.4 us; the launch traced here: 74.9 us
  blocking collectives  28.3 us (38%)
  starting transfers between devices  27.2 us (36%)
  Pallas kernels  17 us (23%)
  local copies, waits for them, and re-layouts  1.52 us (2%)
  between operations  0.91 us (1%)
    all_gather x1, blocking collectives, shards(): tab = lax.all_gather(jnp.stack([keep, got[:ROWS]]), 'rhs')  28.3 us
    all_to_all x1, starting transfers between devices, shards(): win = lax.all_to_all(win, ('box', 'samp'), 0, 0, tiled=True)  12.7 us
    pallas_call x1, Pallas kernels, shards(): call(lower_kernel, [VMEM] * 4, [((64, 8, LANES), F32)], [pltpu.VMEM((2560...  6.96 us
    ppermute x1, starting transfers between devices, shards(): lax.ppermute(rim_oth, both, [(i, flat(s, 1)) for i, s in down] + [(i, fla...  5.63 us
    ppermute x1, starting transfers between devices, shards(): other = lax.ppermute(oth, 'box', [(0, 1), (1, 0)])  3.49 us
    ppermute x1, starting transfers between devices, shards(): got = lax.ppermute(give, 'box', [(0, 1), (1, 0)])  3.4 us
    pallas_call x1, Pallas kernels, shards(): call(ready_kernel, [HBM] * 4, made, [pltpu.VMEM((4, 2, 2, 4096), F32), pl...  3.25 us
    pallas_call x1, Pallas kernels, shards(): call(upper_kernel, [VMEM] * 5 + [HBM] * 4, [part, part, rim, rim], [pltpu...  2.91 us
  transfers between devices with their start and end apart: 5, of which 0 were waited for; matrix products, arithmetic and copies ran while one was open for 0% of the time, Pallas kernels for 14%

commit v1 on v0

v1 whole, which is shorter than its diff:
```python
import jax
import jax.numpy as jnp
from jax import lax
from jax.experimental import pallas as pl
from jax.experimental.pallas import tpu as pltpu
from jax.sharding import PartitionSpec as P

F32, BF16, I32 = jnp.float32, jnp.bfloat16, jnp.int32
VMEM = pl.BlockSpec(memory_space=pltpu.VMEM)
SMEM = pl.BlockSpec(memory_space=pltpu.SMEM)
HBM = pl.BlockSpec(memory_space=pltpu.HBM)
LANES = 128
ROWS = 120
ALL_VMEM = 63 << 20
SENT = ROWS + 16


def call(kernel, ins, outs, scratch=(), flops=0, moved=0, out_place=VMEM, room=24 << 20):
    return pl.pallas_call(
        kernel,
        in_specs=list(ins),
        out_specs=[out_place] * len(outs),
        out_shape=[jax.ShapeDtypeStruct(s, d) for s, d in outs],
        scratch_shapes=list(scratch),
        compiler_params=pltpu.CompilerParams(vmem_limit_bytes=room),
        cost_estimate=pl.CostEstimate(flops=flops, bytes_accessed=moved, transcendentals=0),
    )


def halves(x):
    high = x.astype(BF16)
    return high, (x - high.astype(F32)).astype(BF16)


def row_of(shape=(8, LANES)):
    return lax.broadcasted_iota(I32, shape, 0)


def lane_of(shape=(8, LANES)):
    return lax.broadcasted_iota(I32, shape, 1)


def run_all(copies):
    for copy in copies:
        copy.start()
    for copy in copies:
        copy.wait()


def repeat(count, step, body):
    def several(n, carry):
        for i in range(step):
            body(n * step + i)
        return carry

    lax.fori_loop(0, count // step, several, 0)


def swap(x):
    return jnp.where(row_of() % 2 == 0, pltpu.roll(x, 7, 0), pltpu.roll(x, 1, 0))


def across(x, row):
    return jnp.broadcast_to(x[row : row + 1, :], (8, LANES))


def product3(left, right, dims):
    (lh, ll), (rh, rl) = left, right
    dot = lambda a, b: lax.dot_general(a, b, (dims, ((), ())), preferred_element_type=F32)
    return dot(lh, rh) + (dot(lh, rl) + dot(ll, rh))


def block_of(n):
    return (lax.bitwise_xor(n % 2, lax.axis_index("box")) * 8 + n // 2) * 160


def table_kernel(
    low_hbm, high_hbm, sources_hbm, operators_hbm, pair, give, low, high, sources, operators, sem
):
    half = lax.axis_index("box")
    run_all(
        [
            pltpu.make_async_copy(low_hbm, low, sem.at[0]),
            pltpu.make_async_copy(high_hbm, high, sem.at[1]),
            pltpu.make_async_copy(sources_hbm, sources, sem.at[2]),
            pltpu.make_async_copy(operators_hbm, operators, sem.at[3]),
        ]
    )
    for out, b in ((give, 1 - half), (pair.at[0], half)):
        for op in range(20):
            for jh in range(2):
                lanes = pl.ds(pl.multiple_of((2 * b + jh) * LANES, LANES), LANES)
                at = 4 * op + 2 * jh
                out[at : at + 2, :] = high[op, :, lanes]
            out[80 + 2 * op : 82 + 2 * op, :] = low[op]
    give[ROWS:, :] = jnp.zeros((16, LANES), F32)
    give[ROWS:, 0:16] = sources[...].astype(F32)
    give[ROWS:, 16:32] = operators[...].astype(F32)


def ready_kernel(
    rad_hbm, index, weight, angle, sources_hbm, operators_hbm,
    win_out, w_out, m_out, spin_out,
    rad, rows, win, idx, wgt, ang, w, m, spins, sources, operators, sem, out_sem,
):
    seg, half = lax.axis_index("samp"), lax.axis_index("box")
    start = pl.multiple_of(seg * 512, LANES)
    total = index.shape[1]
    before = pl.multiple_of(jnp.maximum(start - LANES, 0), LANES)
    after = pl.multiple_of(jnp.minimum(start + 512, total - LANES), LANES)
    first = pltpu.make_async_copy(rad_hbm, rad, sem.at[9])
    first.start()
    copies = []
    for n, (src, dst) in enumerate(((index, idx), (weight, wgt), (angle, ang))):
        for k, (at, to, width) in enumerate(((before, 0, 128), (start, 128, 512), (after, 640, 128))):
            copies.append(
                pltpu.make_async_copy(
                    src.at[:, pl.ds(at, width)], dst.at[:, to : to + width], sem.at[3 * n + k]
                )
            )
    copies.append(pltpu.make_async_copy(sources_hbm, sources, sem.at[10]))
    copies.append(pltpu.make_async_copy(operators_hbm, operators, sem.at[11]))
    for copy in copies:
        copy.start()
    first.wait()
    for o in range(4):
        for r in range(2):
            rows[4 * o + 2 * r : 4 * o + 2 * r + 2, :] = rad[o, r]
    n_samp = rows.shape[1] // LANES
    lane = lane_of((16, LANES))
    lane8 = lane_of()
    block = lambda s: rows[:, (s % n_samp) * LANES : (s % n_samp + 1) * LANES]
    for s in range(n_samp):
        here = block(s)
        near_rows, far_rows = here[:8], pltpu.roll(here[8:], 64, 1)
        for b, near, low, rest in ((0, s - 1, 0, 96), (1, s + 1, 32, 128)):
            inside = (lane >= low) & (lane < rest)
            inside8 = (lane8 >= low) & (lane8 < rest)
            win[b * n_samp + s, :16, :] = jnp.where(inside, here, block(near))
            win[b * n_samp + s, 16:, :] = jnp.where(inside8, far_rows, near_rows)
    last = [pltpu.make_async_copy(win, win_out, out_sem.at[0])]
    last[0].start()
    for copy in copies:
        copy.wait()
    slot = lax.broadcasted_iota(I32, (LANES, LANES), 0)

    def band(at, first):
        at = pl.multiple_of(at, LANES)
        found = idx[:, pl.ds(at, LANES)]
        found = found & 127 if first is None else found - first
        value = wgt[:, pl.ds(at, LANES)]
        matrix = jnp.zeros((LANES, LANES), F32)
        for p in range(16):
            matrix += jnp.where(found[p : p + 1, :] == slot, value[p : p + 1, :], 0.0)
        return halves(matrix)

    own = pl.multiple_of(LANES + 256 * half, LANES)

    def interp(n):
        at = pl.multiple_of(n * LANES, LANES)
        w[:LANES, pl.ds(at, LANES)], w[LANES:, pl.ds(at, LANES)] = band(own + at, None)

    def anterp(n):
        at = pl.multiple_of(n * LANES, LANES)
        m[:LANES, pl.ds(at, LANES)], m[LANES:, pl.ds(at, LANES)] = band(at, seg * 128)

    cosine, sine = jnp.cos(ang[...]), jnp.sin(ang[...])
    spin = jnp.where(row_of((4, 768)) % 2 == 0, 1.0, -1.0)
    spins[:32, :] = jnp.concatenate(
        [jnp.broadcast_to(cosine[o : o + 1], (4, 768)) for o in range(8)], 0
    )
    spins[32:64, :] = jnp.concatenate(
        [jnp.broadcast_to(sine[o : o + 1], (4, 768)) * spin for o in range(8)], 0
    )
    spins[64:, :] = jnp.zeros((16, 768), F32)
    spins[64:, 0:16] = sources[...].astype(F32)
    spins[64:, 16:32] = operators[...].astype(F32)

    def send(src, dst):
        last.append(pltpu.make_async_copy(src, dst, out_sem.at[len(last)]))
        last[-1].start()

    send(spins, spin_out)
    repeat(2, 2, interp)
    send(w, w_out)
    repeat(6, 2, anterp)
    send(m, m_out)
    for copy in last:
        copy.wait()


def upper_kernel(
    tab, got, win, w_in, spin_in,
    own, oth, rim_own, rim_oth,
    tre, tim, full, pat, same, cross, w, spins, lists, scalars, sem,
):
    half = lax.axis_index("box")
    lanes = pl.ds(pl.multiple_of(LANES + 256 * half, LANES), 256)
    copies = [
        pltpu.make_async_copy(spin_in.at[pl.ds(64, 16), pl.ds(0, LANES)], spins.at[64:, 0:LANES], sem.at[0]),
        pltpu.make_async_copy(w_in, w, sem.at[1]),
        pltpu.make_async_copy(spin_in.at[pl.ds(0, 64), lanes], spins.at[0:64, :], sem.at[2]),
    ]
    for copy in copies:
        copy.start()
    lists[16:, :] = (got[ROWS:, :] * 8.0).astype(I32)
    copies[0].wait()
    lists[:16, :] = (spins[64:, :LANES] * 8.0).astype(I32)
    listed = pltpu.make_async_copy(lists, scalars, sem.at[3])
    listed.start()
    row = row_of()
    upper = row < 4
    flip = jnp.where(row % 2 == 0, 1.0, -1.0)

    def device(n):
        first = block_of(n)
        for i in range(20):
            four = tab[n, 4 * i : 4 * i + 4, :]
            at = pl.multiple_of(first + 8 * i, 8)
            tre[pl.ds(at, 8), :] = jnp.where(upper, across(four, 0), across(four, 2))
            tim[pl.ds(at, 8), :] = jnp.where(upper, across(four, 1), across(four, 3)) * flip

    repeat(16, 2, device)
    copies[1].wait()

    def interpolate(n):
        at = pl.multiple_of(n * 128, 128)
        rows = jnp.concatenate([win[n * 8 + q, :16, :] for q in range(8)], 0)
        full[pl.ds(at, 128), :] = product3(halves(rows), (w[:LANES], w[LANES:]), ((1,), (0,)))

    repeat(8, 4, interpolate)
    copies[2].wait()

    def aggregate(u):
        at = pl.multiple_of(u * 32, 32)
        lay = []
        for h in range(2):
            lanes = slice(h * LANES, (h + 1) * LANES)
            straight = turned = 0.0
            for k in range(4):
                x = full[pl.ds(at + 8 * k, 8), lanes]
                straight += spins[8 * k : 8 * k + 8, lanes] * x
                turned += spins[32 + 8 * k : 40 + 8 * k, lanes] * x
            total = straight + swap(turned)
            lay.append(total + pltpu.roll(total, 4, 0))
        pat[pl.ds(pl.multiple_of(u * 8, 8), 8), :] = jnp.where(upper, lay[0], lay[1])

    repeat(32, 4, aggregate)
    listed.wait()

    def translate(n):
        for q in range(2):
            u = 2 * n + q
            acc = jnp.zeros((8, LANES), F32)
            acc2 = jnp.zeros((8, LANES), F32)
            for e in range(16):
                x = pat[pl.ds(pl.multiple_of(scalars[u, e], 8), 8), :]
                op = pl.ds(pl.multiple_of(scalars[u, 16 + e], 8), 8)
                acc += tre[op, :] * x
                acc2 += tim[op, :] * x
            same[u], cross[u] = acc, acc2

    repeat(16, 2, translate)

    def border(n):
        for whole, rim, shift in ((own, rim_own, 0), (oth, rim_oth, 16)):
            one = same[2 * n + shift] + swap(cross[2 * n + shift])
            two = same[2 * n + 1 + shift] + swap(cross[2 * n + 1 + shift])
            whole[2 * n], whole[2 * n + 1] = one, two
            first = jnp.where(upper, one, pltpu.roll(two, 4, 0))
            last = jnp.where(upper, pltpu.roll(one, 4, 0), two)
            rim[n] = jnp.where(half == 0, first, last)

    repeat(8, 8, border)


def lower_kernel(sources, operators, win, tab, out, t8, pat, full, lists, scalars, sem):
    by_target = [jnp.transpose(x[...] * 8) for x in (sources, operators)]
    for q in range(4):
        for k in range(2):
            lists[:, 32 * q + 16 * k : 32 * q + 16 * k + 16] = by_target[k][32 * q : 32 * q + 32]
    listed = pltpu.make_async_copy(lists, scalars, sem)
    listed.start()
    row, lane = row_of(), lane_of()
    upper, lane_half = row < 4, lax.axis_index("box") * 96
    flip = jnp.where(upper | (row % 2 == 0), 1.0, -1.0)
    absent = (lane >= 96 - lane_half) & (lane < 128 - lane_half)

    def device(n):
        first = block_of(n)
        for i in range(20):
            two = tab[n, 80 + 2 * i : 82 + 2 * i, :]
            at = pl.multiple_of(first + 8 * i, 8)
            t8[pl.ds(at, 8), :] = jnp.where(upper, across(two, 0), across(two, 1)) * flip

    repeat(16, 2, device)
    def spread_out(n):
        extra = win[n, 16:24, :]
        for v, x in enumerate((extra, pltpu.roll(extra, 64, 1))):
            x = jnp.where(absent, x, win[n, 8 * v : 8 * v + 8, :])
            turned = pltpu.roll(x, 4, 0)
            at = pl.multiple_of(n * 32 + 16 * v, 8)
            pat[pl.ds(at, 8), :] = jnp.where(upper, x, turned)
            pat[pl.ds(at + 8, 8), :] = jnp.where(upper, turned, x)

    repeat(64, 8, spread_out)
    listed.wait()

    def four(n):
        for q in range(4):
            acc = [jnp.zeros((8, LANES), F32)] * 2
            for e in range(16):
                op = pl.ds(pl.multiple_of(scalars[n, 32 * q + 16 + e], 8), 8)
                src = pl.ds(pl.multiple_of(scalars[n, 32 * q + e], 8), 8)
                acc[e % 2] += t8[op, :] * pat[src, :]
            full[32 * q + n] = acc[0] + acc[1]

    repeat(32, 1, four)

    def fold(n):
        one, two = full[2 * n], full[2 * n + 1]
        same = jnp.where(upper, one, pltpu.roll(two, 4, 0))
        out[n] = same + swap(jnp.where(upper, pltpu.roll(one, 4, 0), two))

    repeat(64, 16, fold)


def final_kernel(
    own, got, rim_a, rim_b, low, m, spins, low_out, high_out, lh, ll
):
    row = row_of()
    upper = row < 4
    first = lax.axis_index("box") == 0

    def pair(n):
        rims = (jnp.where(first, rim_b[n], rim_a[n]), jnp.where(first, rim_a[n], rim_b[n]))
        for q in range(2):
            u = 2 * n + q
            one = jnp.where(first, own[u], got[u])
            two = jnp.where(first, got[u], own[u])
            for jt, x in enumerate((one, one, two, two)):
                for r in range(2):
                    high_out[u, r, :, jt * LANES : (jt + 1) * LANES] = x[
                        4 * (jt % 2) + 2 * r : 4 * (jt % 2) + 2 * r + 2, :
                    ]
            blocks = []
            for x in (one, two):
                turned = pltpu.roll(x, 4, 0)
                blocks += [jnp.where(upper, x, turned), jnp.where(upper, turned, x)]
            edge = []
            for x in rims:
                turned = pltpu.roll(x, 4, 0)
                edge.append(jnp.where(upper, x, turned) if q == 0 else jnp.where(upper, turned, x))
            blocks = [edge[0]] + blocks + [edge[1]]
            at = pl.multiple_of(u * 32, 32)
            for jt, x in enumerate(blocks):
                lanes = slice(jt * LANES, (jt + 1) * LANES)
                y = swap(x)
                rows = jnp.concatenate(
                    [
                        spins[8 * g : 8 * g + 8, lanes] * x + spins[32 + 8 * g : 40 + 8 * g, lanes] * y
                        for g in range(4)
                    ],
                    0,
                )
                lh[pl.ds(at, 32), lanes], ll[pl.ds(at, 32), lanes] = halves(rows)

    repeat(8, 2, pair)

    def block(n):
        at = pl.multiple_of(n * 128, 128)
        sums = product3(
            (lh[pl.ds(at, 128), :], ll[pl.ds(at, 128), :]), (m[:LANES, :], m[LANES:, :]), ((1,), (1,))
        )
        low_out[pl.ds(at, 128), :] = sums + low[pl.ds(at, 128), :]

    repeat(4, 2, block)


def shards(
    radiated,
    low_table,
    high_table,
    low_sources,
    low_operators,
    high_sources,
    high_operators,
    stencil_index,
    stencil_weight,
    shift_angle,
):
    n_samp = lax.axis_size("samp")
    dma = pltpu.SemaphoreType.DMA
    pair, give = call(
        table_kernel,
        [HBM] * 4,
        [((2, ROWS, LANES), F32), ((SENT, LANES), F32)],
        [pltpu.VMEM((20, 2, LANES), F32), pltpu.VMEM((20, 2, 512), F32)]
        + [pltpu.VMEM((16, 16), I32)] * 2
        + [dma((4,))],
        moved=1 << 20,
        room=ALL_VMEM,
    )(low_table, high_table, high_sources, high_operators)
    got = lax.ppermute(give, "box", [(0, 1), (1, 0)])
    made = [
        ((64, 24, LANES), F32),
        ((256, 256), BF16),
        ((256, 768), BF16),
        ((80, 768), F32),
    ]
    win, w, m, spins = call(
        ready_kernel,
        [HBM] * 6,
        made,
        [pltpu.VMEM((4, 2, 2, 4096), F32), pltpu.VMEM((16, 4096), F32), pltpu.VMEM(*made[0])]
        + [pltpu.VMEM((16, 768), I32), pltpu.VMEM((16, 768), F32), pltpu.VMEM((8, 768), F32)]
        + [pltpu.VMEM(*x) for x in made[1:]]
        + [pltpu.VMEM((16, 16), I32)] * 2
        + [dma((12,)), dma((4,))],
        flops=10 << 20,
        moved=8 << 20,
        out_place=HBM,
        room=ALL_VMEM,
    )(radiated, stencil_index, stencil_weight, shift_angle, high_sources, high_operators)
    win, got = lax.optimization_barrier((win, got))
    win = lax.all_to_all(win, ("box", "samp"), 0, 0, tiled=True)
    tab = lax.all_gather(pair.at[1].set(got[:ROWS]), "rhs", tiled=True)
    part, rim = ((16, 8, LANES), F32), ((8, 8, LANES), F32)
    own, oth, rim_own, rim_oth = call(
        upper_kernel,
        [VMEM] * 3 + [HBM] * 2,
        [part, part, rim, rim],
        [
            pltpu.VMEM((2560, LANES), F32),
            pltpu.VMEM((2560, LANES), F32),
            pltpu.VMEM((1024, 256), F32),
            pltpu.VMEM((256, LANES), F32),
            pltpu.VMEM((32, 8, LANES), F32),
            pltpu.VMEM((32, 8, LANES), F32),
            pltpu.VMEM(*made[1]),
            pltpu.VMEM((80, 256), F32),
            pltpu.VMEM((32, LANES), I32),
            pltpu.SMEM((32, LANES), I32),
            dma((4,)),
        ],
        flops=200 << 20,
        moved=6 << 20,
    )(tab, got, win, w, spins)
    flat = lambda s, b: 2 * s + b
    other = lax.ppermute(oth, "box", [(0, 1), (1, 0)])
    down = [(flat(s, 0), s - 1) for s in range(1, n_samp)]
    up = [(flat(s, 1), s + 1) for s in range(n_samp - 1)]
    both = ("samp", "box")
    rim_a = lax.ppermute(
        rim_own, both, [(i, flat(s, 0)) for i, s in down] + [(i, flat(s, 1)) for i, s in up]
    )
    rim_b = lax.ppermute(
        rim_oth, both, [(i, flat(s, 1)) for i, s in down] + [(i, flat(s, 0)) for i, s in up]
    )
    (low,) = call(
        lower_kernel,
        [VMEM] * 4,
        [((64, 8, LANES), F32)],
        [
            pltpu.VMEM((2560, LANES), F32),
            pltpu.VMEM((2048, LANES), F32),
            pltpu.VMEM((LANES, 8, LANES), F32),
            pltpu.VMEM((32, LANES), I32),
            pltpu.SMEM((32, LANES), I32),
            dma,
        ],
        flops=20 << 20,
        moved=10 << 20,
    )(low_sources.T, low_operators.T, win, tab)
    low_incoming, high_incoming = call(
        final_kernel,
        [VMEM] * 7,
        [((512, LANES), F32), ((16, 2, 2, 512), F32)],
        [pltpu.VMEM((512, 768), BF16), pltpu.VMEM((512, 768), BF16)],
        flops=300 << 20,
        moved=4 << 20,
    )(own, other, rim_a, rim_b, low.reshape(512, LANES), m, spins)
    return low_incoming.reshape(128, 2, 2, LANES), high_incoming


def solution(mesh):
    return jax.shard_map(
        shards,
        mesh=mesh,
        in_specs=(
            P(("box", "samp"), "rhs", None, None),
            P(("box", "rhs"), None, "samp"),
            P(("box", "rhs"), None, "samp"),
            P("box", None),
            P("box", None),
            P("box", None),
            P("box", None),
            P(),
            P(),
            P(),
        ),
        out_specs=(P("box", "rhs", None, "samp"), P("box", "rhs", None, "samp")),
        check_vma=False,
    )
```

time: 75.4 us -> 71.3 us (0.946)
  Pallas kernels: 17 us -> 14.5 us
  local copies, waits for them, and re-layouts: 1.52 us -> 0.04 us
    pallas_call x1, Pallas kernels: 6.96 us -> 4.6 us  [shards(): call(lower_kernel, [VMEM] * 4, [((64, 8, LANES), F32)], [pltpu.VMEM((2560...]
    unnamed x26 -> x12, local copies, waits for them, and re-layouts: 1.51 us -> 0.03 us
  transfers between devices with their start and end apart: 5 -> 5, of which waited for: 0 -> 0; matrix products, arithmetic and copies ran while one was open for 0% -> 0% of each run, Pallas kernels for 14% -> 11%
where the time goes in v1:
time: 71.3 us; the launch traced here: 71 us
  blocking collectives  28.3 us (40%)
  starting transfers between devices  27.3 us (38%)
  Pallas kernels  14.5 us (20%)
  between operations  0.82 us (1%)
    all_gather x1, blocking collectives, shards(): tab = lax.all_gather(pair.at[1].set(got[:ROWS]), 'rhs', tiled=True)  28.3 us
    all_to_all x1, starting transfers between devices, shards(): win = lax.all_to_all(win, ('box', 'samp'), 0, 0, tiled=True)  12.8 us
    ppermute x1, starting transfers between devices, shards(): lax.ppermute(rim_oth, both, [(i, flat(s, 1)) for i, s in down] + [(i, fla...  5.63 us
    pallas_call x1, Pallas kernels, shards(): call(lower_kernel, [VMEM] * 4, [((64, 8, LANES), F32)], [pltpu.VMEM((2560...  4.6 us
    ppermute x1, starting transfers between devices, shards(): other = lax.ppermute(oth, 'box', [(0, 1), (1, 0)])  3.49 us
    ppermute x1, starting transfers between devices, shards(): got = lax.ppermute(give, 'box', [(0, 1), (1, 0)])  3.4 us
    pallas_call x1, Pallas kernels, shards(): call(ready_kernel, [HBM] * 6, made, [pltpu.VMEM((4, 2, 2, 4096), F32), pl...  3.29 us
    pallas_call x1, Pallas kernels, shards(): call(upper_kernel, [VMEM] * 3 + [HBM] * 2, [part, part, rim, rim], [pltpu...  2.69 us
  transfers between devices with their start and end apart: 5, of which 0 were waited for; matrix products, arithmetic and copies ran while one was open for 0% of the time, Pallas kernels for 11%

profile of v1, /device:TPU:64, one launch (start us, length us, event | category | flops | bytes accessed | tf_op | source)
XLA Modules:
  0.0 71.0 jit_solution(8284239414210487670)
XLA Ops:
  0.6 1.7 %shard_map.113 = (f32[2,120,128]{2,1,0:T(8,128)}, f32[136,128]{1,0:T(8,128)}) custom-call(f32[20,2,128]{2,1,0:T(2,128)} %low_hbm.1, f32[20,2,512]{2,1,0:T(2,128)} %high_hbm.1, s32[16,16]{1,0:T(8,128)} %sources_hbm.3, s32[16,16]{1,0:T(8,128)} %operators_hbm.3), custom_call_target="tpu_custom_call" | custom-call | bytes 1048576 | tf_op jit(solution)/shard_map/pallas_call | solution.py:394
  2.3 3.4 %collective-permute-start = (f32[136,128]{1,0:T(8,128)}, f32[136,128]{1,0:T(8,128)S(1)}, u32[]{:S(2)}, u32[]{:S(2)}) collective-permute-start(f32[136,128]{1,0:T(8,128)} %get-tuple-element.30), channel_id=1, source_target_pairs={{0,8},{8,0},{1,9},{9,1},{2,10},{10,2},{3,11},{11,3},{4,12},{12,4},... | collective-permute-start | bytes 208904 | tf_op jit(solution)/shard_map/ppermute | solution.py:404
  5.7 3.3 %shard_map.114 = (f32[64,24,128]{2,1,0:T(8,128)}, bf16[256,256]{1,0:T(8,128)(2,1)}, bf16[256,768]{1,0:T(8,128)(2,1)}, f32[80,768]{1,0:T(8,128)}) custom-call(f32[4,2,2,4096]{3,2,1,0:T(2,128)} %rad_hbm.1, s32[16,16384]{1,0:T(8,128)} %index.1, f32[16,16384]{1,0:T(8,128)} %weight.1, f32[8,16384]{1,0:T(8,128)} %angle.1, s32[16,16]{1,0:T(8,128)} %sources_hbm.3, ...), custom_call_target="tpu_custom_call" | custom-call | flops 10485760 | bytes 8388608 | tf_op jit(solution)/shard_map/pallas_call | solution.py:411
  9.0 0.0 collective-permute-done.got
  9.0 0.0 copy-start.5
  9.0 12.8 %all-to-all-start = ((f32[64,24,128]{2,1,0:T(8,128)}), f32[64,24,128]{2,1,0:T(8,128)S(1)}, u32[]{:S(2)}, u32[]{:S(2)}) async-start(f32[64,24,128]{2,1,0:T(8,128)} %get-tuple-element.32), calls=%async_computation | async-start | bytes 1572864 | tf_op jit(solution)/shard_map/all_to_all | solution.py:426
  21.9 0.0 copy-done.5
  21.9 0.0 copy-start
  21.9 0.0 copy-start.1
  21.9 28.3 %all_gather.3.tab = f32[16,120,128]{2,1,0:T(8,128)S(1)} all-gather(f32[2,120,128]{2,1,0:T(8,128)S(1)} %bitcast_dynamic-update-slice_fusion), channel_id=1, replica_groups=mesh['samp'=32,'box'=2,'rhs'=8] {'rhs'}, dimensions={0}, use_global_device_ids=true | all-gather | bytes 1105920 | tf_op jit(solution)/shard_map/all_gather | solution.py:427
  50.2 0.0 all-to-all-done.win
  50.2 0.0 copy-done
  50.2 0.0 copy-done.1
  50.2 0.0 copy-start.3
  50.2 2.7 %shard_map.115 = (f32[16,8,128]{2,1,0:T(8,128)S(1)}, f32[16,8,128]{2,1,0:T(8,128)S(1)}, f32[8,8,128]{2,1,0:T(8,128)S(1)}, f32[8,8,128]{2,1,0:T(8,128)S(1)}) custom-call(f32[16,120,128]{2,1,0:T(8,128)S(1)} %all_gather.3.tab, f32[136,128]{1,0:T(8,128)S(1)} %collective-permute-done.got, f32[64,24,128]{2,1,0:T(8,128)S(1)} %all-to-all-done.win, ...), custom_call_target="tpu_custom_call" | custom-call | flops 209715200 | bytes 6291456 | tf_op jit(solution)/shard_map/pallas_call | solution.py:429
  52.9 0.0 copy-start.2
  53.0 3.5 %collective-permute-start.1 = (f32[16,8,128]{2,1,0:T(8,128)S(1)}, f32[16,8,128]{2,1,0:T(8,128)S(1)}, u32[]{:S(2)}, u32[]{:S(2)}) collective-permute-start(f32[16,8,128]{2,1,0:T(8,128)S(1)} %get-tuple-element.36), channel_id=1, source_target_pairs={{0,8},{8,0},{1,9},{9,1},{2,10},{10,2},{3,11},{11,3},{4,12},{12,4},... | collective-permute-start | bytes 196616 | tf_op jit(solution)/shard_map/ppermute | solution.py:450
  56.5 1.9 %collective-permute-start.2 = (f32[8,8,128]{2,1,0:T(8,128)S(1)}, f32[8,8,128]{2,1,0:T(8,128)S(1)}, u32[]{:S(2)}, u32[]{:S(2)}) collective-permute-start(f32[8,8,128]{2,1,0:T(8,128)S(1)} %get-tuple-element.37), channel_id=1, source_target_pairs={{16,0},{32,16},{48,32},{64,48},{80,64},{96,80},{112,96},{128,112},... | collective-permute-start | bytes 98312 | tf_op jit(solution)/shard_map/ppermute | solution.py:454
  58.4 5.6 %collective-permute-start.3 = (f32[8,8,128]{2,1,0:T(8,128)S(1)}, f32[8,8,128]{2,1,0:T(8,128)S(1)}, u32[]{:S(2)}, u32[]{:S(2)}) collective-permute-start(f32[8,8,128]{2,1,0:T(8,128)S(1)} %get-tuple-element.38), channel_id=1, source_target_pairs={{16,8},{32,24},{48,40},{64,56},{80,72},{96,88},{112,104},{128,120}... | collective-permute-start | bytes 98312 | tf_op jit(solution)/shard_map/ppermute | solution.py:457
  64.0 0.0 copy-done.3
  64.0 0.0 copy-done.2
  64.0 0.0 copy-start.4
  64.1 4.6 %shard_map.116 = f32[64,8,128]{2,1,0:T(8,128)S(1)} custom-call(s32[16,128]{1,0:T(8,128)S(1)} %bitcast.7, s32[16,128]{1,0:T(8,128)S(1)} %bitcast.8, f32[64,24,128]{2,1,0:T(8,128)S(1)} %all-to-all-done.win, f32[16,120,128]{2,1,0:T(8,128)S(1)} %all_gather.3.tab), custom_call_target="tpu_custom_call" | custom-call | flops 20971520 | bytes 10485760 | tf_op jit(solution)/shard_map/pallas_call | solution.py:460
  68.7 0.0 collective-permute-done.2.rim_a
  68.7 0.0 collective-permute-done.3.rim_b
  68.7 0.0 collective-permute-done.1.got
  68.7 0.0 copy-done.4
  68.7 2.3 %shard_map.117 = (f32[512,128]{1,0:T(8,128)}, f32[16,2,2,512]{3,2,1,0:T(2,128)}) custom-call(f32[16,8,128]{2,1,0:T(8,128)S(1)} %get-tuple-element.35.own, f32[16,8,128]{2,1,0:T(8,128)S(1)} %collective-permute-done.1.got, f32[8,8,128]{2,1,0:T(8,128)S(1)} %collective-permute-done.2.rim_a, f32[8,8,128]{2,1,0:T(8,128)S(1)} %collective-permute-done.3.rim_b, ...), custom_call_target="tpu_custom_call" | custom-call | flops 314572800 | bytes 4194304 | tf_op jit(solution)/shard_map/pallas_call | solution.py:475
  (1 shorter events, 0.0 us)
Async XLA Ops:
  2.3 6.7 %collective-permute-start = (f32[136,128]{1,0:T(8,128)}, f32[136,128]{1,0:T(8,128)S(1)}, u32[]{:S(2)}, u32[]{:S(2)}) collective-permute-start(f32[136,128]{1,0:T(8,128)} %get-tuple-element.30), channel_id=1, source_target_pairs={{0,8},{8,0},{1,9},{9,1},{2,10},{10,2},{3,11},{11,3},{4,12},{12,4},... | collective-permute-start | bytes 208904 | tf_op jit(solution)/shard_map/ppermute | solution.py:404
  9.0 12.9 %copy-start.5 = (f32[2,120,128]{2,1,0:T(8,128)S(1)}, f32[2,120,128]{2,1,0:T(8,128)}, u32[]{:S(2)}) copy-start(f32[2,120,128]{2,1,0:T(8,128)} %get-tuple-element.28) | copy-start | bytes 368644
  9.0 41.2 %all-to-all-start = ((f32[64,24,128]{2,1,0:T(8,128)}), f32[64,24,128]{2,1,0:T(8,128)S(1)}, u32[]{:S(2)}, u32[]{:S(2)}) async-start(f32[64,24,128]{2,1,0:T(8,128)} %get-tuple-element.32), calls=%async_computation | async-start | bytes 1572864 | tf_op jit(solution)/shard_map/all_to_all | solution.py:426
  21.9 28.3 %copy-start = (f32[80,768]{1,0:T(8,128)S(1)}, f32[80,768]{1,0:T(8,128)}, u32[]{:S(2)}) copy-start(f32[80,768]{1,0:T(8,128)} %get-tuple-element.34.spin_in.spins) | copy-start | bytes 737284
  21.9 28.3 %copy-start.1 = (bf16[256,256]{1,0:T(8,128)(2,1)S(1)}, bf16[256,256]{1,0:T(8,128)(2,1)}, u32[]{:S(2)}) copy-start(bf16[256,256]{1,0:T(8,128)(2,1)} %get-tuple-element.33.w_in) | copy-start | bytes 393220
  50.2 13.8 %copy-start.3 = (s32[128,16]{0,1:T(8,128)S(1)}, s32[128,16]{0,1:T(8,128)}, u32[]{:S(2)}) copy-start(s32[128,16]{0,1:T(8,128)} %param.16) | copy-start | bytes 24580
  52.9 11.1 %copy-start.2 = (s32[128,16]{0,1:T(8,128)S(1)}, s32[128,16]{0,1:T(8,128)}, u32[]{:S(2)}) copy-start(s32[128,16]{0,1:T(8,128)} %param.15) | copy-start | bytes 24580
  53.0 15.7 %collective-permute-start.1 = (f32[16,8,128]{2,1,0:T(8,128)S(1)}, f32[16,8,128]{2,1,0:T(8,128)S(1)}, u32[]{:S(2)}, u32[]{:S(2)}) collective-permute-start(f32[16,8,128]{2,1,0:T(8,128)S(1)} %get-tuple-element.36), channel_id=1, source_target_pairs={{0,8},{8,0},{1,9},{9,1},{2,10},{10,2},{3,11},{11,3},{4,12},{12,4},... | collective-permute-start | bytes 196616 | tf_op jit(solution)/shard_map/ppermute | solution.py:450
  56.5 12.2 %collective-permute-start.2 = (f32[8,8,128]{2,1,0:T(8,128)S(1)}, f32[8,8,128]{2,1,0:T(8,128)S(1)}, u32[]{:S(2)}, u32[]{:S(2)}) collective-permute-start(f32[8,8,128]{2,1,0:T(8,128)S(1)} %get-tuple-element.37), channel_id=1, source_target_pairs={{16,0},{32,16},{48,32},{64,48},{80,64},{96,80},{112,96},{128,112},... | collective-permute-start | bytes 98312 | tf_op jit(solution)/shard_map/ppermute | solution.py:454
  58.4 10.3 %collective-permute-start.3 = (f32[8,8,128]{2,1,0:T(8,128)S(1)}, f32[8,8,128]{2,1,0:T(8,128)S(1)}, u32[]{:S(2)}, u32[]{:S(2)}) collective-permute-start(f32[8,8,128]{2,1,0:T(8,128)S(1)} %get-tuple-element.38), channel_id=1, source_target_pairs={{16,8},{32,24},{48,40},{64,56},{80,72},{96,88},{112,104},{128,120}... | collective-permute-start | bytes 98312 | tf_op jit(solution)/shard_map/ppermute | solution.py:457
  64.0 4.6 %copy-start.4 = (bf16[256,768]{1,0:T(8,128)(2,1)S(1)}, bf16[256,768]{1,0:T(8,128)(2,1)}, u32[]{:S(2)}) copy-start(bf16[256,768]{1,0:T(8,128)(2,1)} %get-tuple-element.39.m) | copy-start | bytes 1179652

commit v2 on v1

--- a/solution.py
+++ b/solution.py
@@ -74,10 +74,18 @@
     return (lax.bitwise_xor(n % 2, lax.axis_index("box")) * 8 + n // 2) * 160
 
 
+def pack_tables(low, high, b, out):
+    for op in range(20):
+        for jh in range(2):
+            lanes = pl.ds(pl.multiple_of((2 * b + jh) * LANES, LANES), LANES)
+            at = 4 * op + 2 * jh
+            out[at : at + 2, :] = high[op, :, lanes]
+        out[80 + 2 * op : 82 + 2 * op, :] = low[op]
+
+
 def table_kernel(
-    low_hbm, high_hbm, sources_hbm, operators_hbm, pair, give, low, high, sources, operators, sem
+    low_hbm, high_hbm, sources_hbm, operators_hbm, give, low, high, sources, operators, sem
 ):
-    half = lax.axis_index("box")
     run_all(
         [
             pltpu.make_async_copy(low_hbm, low, sem.at[0]),
@@ -86,22 +94,16 @@
             pltpu.make_async_copy(operators_hbm, operators, sem.at[3]),
         ]
     )
-    for out, b in ((give, 1 - half), (pair.at[0], half)):
-        for op in range(20):
-            for jh in range(2):
-                lanes = pl.ds(pl.multiple_of((2 * b + jh) * LANES, LANES), LANES)
-                at = 4 * op + 2 * jh
-                out[at : at + 2, :] = high[op, :, lanes]
-            out[80 + 2 * op : 82 + 2 * op, :] = low[op]
+    pack_tables(low, high, 1 - lax.axis_index("box"), give)
     give[ROWS:, :] = jnp.zeros((16, LANES), F32)
     give[ROWS:, 0:16] = sources[...].astype(F32)
     give[ROWS:, 16:32] = operators[...].astype(F32)
 
 
 def ready_kernel(
-    rad_hbm, index, weight, angle, sources_hbm, operators_hbm,
-    win_out, w_out, m_out, spin_out,
-    rad, rows, win, idx, wgt, ang, w, m, spins, sources, operators, sem, out_sem,
+    rad_hbm, index, weight, angle, sources_hbm, operators_hbm, low_hbm, high_hbm,
+    win_out, w_out, m_out, spin_out, pair_out,
+    rad, rows, win, idx, wgt, ang, w, m, spins, sources, operators, low_own, high_own, keep, sem, out_sem,
 ):
     seg, half = lax.axis_index("samp"), lax.axis_index("box")
     start = pl.multiple_of(seg * 512, LANES)
@@ -120,6 +122,8 @@
             )
     copies.append(pltpu.make_async_copy(sources_hbm, sources, sem.at[10]))
     copies.append(pltpu.make_async_copy(operators_hbm, operators, sem.at[11]))
+    copies.append(pltpu.make_async_copy(low_hbm, low_own, sem.at[12]))
+    copies.append(pltpu.make_async_copy(high_hbm, high_own, sem.at[13]))
     for copy in copies:
         copy.start()
     first.wait()
@@ -142,27 +146,18 @@
     last[0].start()
     for copy in copies:
         copy.wait()
-    slot = lax.broadcasted_iota(I32, (LANES, LANES), 0)
-
-    def band(at, first):
-        at = pl.multiple_of(at, LANES)
+
+    def band(at, first, low=0, rest=LANES):
         found = idx[:, pl.ds(at, LANES)]
         found = found & 127 if first is None else found - first
         value = wgt[:, pl.ds(at, LANES)]
-        matrix = jnp.zeros((LANES, LANES), F32)
+        matrix = jnp.zeros((rest - low, LANES), F32)
+        slot = row_of((rest - low, LANES)) + low
         for p in range(16):
             matrix += jnp.where(found[p : p + 1, :] == slot, value[p : p + 1, :], 0.0)
         return halves(matrix)
 
     own = pl.multiple_of(LANES + 256 * half, LANES)
-
-    def interp(n):
-        at = pl.multiple_of(n * LANES, LANES)
-        w[:LANES, pl.ds(at, LANES)], w[LANES:, pl.ds(at, LANES)] = band(own + at, None)
-
-    def anterp(n):
-        at = pl.multiple_of(n * LANES, LANES)
-        m[:LANES, pl.ds(at, LANES)], m[LANES:, pl.ds(at, LANES)] = band(at, seg * 128)
 
     cosine, sine = jnp.cos(ang[...]), jnp.sin(ang[...])
     spin = jnp.where(row_of((4, 768)) % 2 == 0, 1.0, -1.0)
@@ -181,32 +176,34 @@
         last[-1].start()
 
     send(spins, spin_out)
-    repeat(2, 2, interp)
+    pack_tables(low_own, high_own, half, keep)
+    send(keep, pair_out.at[0])
+    for n in range(2):
+        lanes = slice(n * LANES, (n + 1) * LANES)
+        w[:LANES, lanes], w[LANES:, lanes] = band(
+            pl.multiple_of(own + n * LANES, LANES), None
+        )
     send(w, w_out)
-    repeat(6, 2, anterp)
+    m[...] = jnp.zeros_like(m)
+    for n in range(6):
+        lanes, low, rest = slice(n * LANES, (n + 1) * LANES), max(32 * n - 64, 0), min(32 * n + 32, LANES)
+        m[low:rest, lanes], m[LANES + low : LANES + rest, lanes] = band(
+            n * LANES, seg * 128, low, rest
+        )
     send(m, m_out)
     for copy in last:
         copy.wait()
 
 
 def upper_kernel(
-    tab, got, win, w_in, spin_in,
+    tab, got, win, w, spins,
     own, oth, rim_own, rim_oth,
-    tre, tim, full, pat, same, cross, w, spins, lists, scalars, sem,
+    tre, tim, full, pat, same, cross, lists, scalars, sem,
 ):
     half = lax.axis_index("box")
-    lanes = pl.ds(pl.multiple_of(LANES + 256 * half, LANES), 256)
-    copies = [
-        pltpu.make_async_copy(spin_in.at[pl.ds(64, 16), pl.ds(0, LANES)], spins.at[64:, 0:LANES], sem.at[0]),
-        pltpu.make_async_copy(w_in, w, sem.at[1]),
-        pltpu.make_async_copy(spin_in.at[pl.ds(0, 64), lanes], spins.at[0:64, :], sem.at[2]),
-    ]
-    for copy in copies:
-        copy.start()
+    lists[:16, :] = (spins[64:, :LANES] * 8.0).astype(I32)
     lists[16:, :] = (got[ROWS:, :] * 8.0).astype(I32)
-    copies[0].wait()
-    lists[:16, :] = (spins[64:, :LANES] * 8.0).astype(I32)
-    listed = pltpu.make_async_copy(lists, scalars, sem.at[3])
+    listed = pltpu.make_async_copy(lists, scalars, sem)
     listed.start()
     row = row_of()
     upper = row < 4
@@ -221,7 +218,6 @@
             tim[pl.ds(at, 8), :] = jnp.where(upper, across(four, 1), across(four, 3)) * flip
 
     repeat(16, 2, device)
-    copies[1].wait()
 
     def interpolate(n):
         at = pl.multiple_of(n * 128, 128)
@@ -229,16 +225,15 @@
         full[pl.ds(at, 128), :] = product3(halves(rows), (w[:LANES], w[LANES:]), ((1,), (0,)))
 
     repeat(8, 4, interpolate)
-    copies[2].wait()
 
     def aggregate(u):
         at = pl.multiple_of(u * 32, 32)
         lay = []
         for h in range(2):
-            lanes = slice(h * LANES, (h + 1) * LANES)
+            lanes = pl.ds(pl.multiple_of((2 * half + 1 + h) * LANES, LANES), LANES)
             straight = turned = 0.0
             for k in range(4):
-                x = full[pl.ds(at + 8 * k, 8), lanes]
+                x = full[pl.ds(at + 8 * k, 8), h * LANES : (h + 1) * LANES]
                 straight += spins[8 * k : 8 * k + 8, lanes] * x
                 turned += spins[32 + 8 * k : 40 + 8 * k, lanes] * x
             total = straight + swap(turned)
@@ -326,7 +321,7 @@
 
 
 def final_kernel(
-    own, got, rim_a, rim_b, low, m, spins, low_out, high_out, lh, ll
+    own, got, rim_a, rim_b, low, m, spins, low_hbm, high_hbm, low_out, high_out, lh, ll, sem
 ):
     row = row_of()
     upper = row < 4
@@ -367,14 +362,16 @@
 
     repeat(8, 2, pair)
 
-    def block(n):
-        at = pl.multiple_of(n * 128, 128)
-        sums = product3(
-            (lh[pl.ds(at, 128), :], ll[pl.ds(at, 128), :]), (m[:LANES, :], m[LANES:, :]), ((1,), (1,))
-        )
-        low_out[pl.ds(at, 128), :] = sums + low[pl.ds(at, 128), :]
-
-    repeat(4, 2, block)
+    copies = [pltpu.make_async_copy(high_out, high_hbm, sem.at[4])]
+    copies[0].start()
+    for n in range(4):
+        at = slice(n * 128, (n + 1) * 128)
+        sums = product3((lh[at, :], ll[at, :]), (m[:LANES, :], m[LANES:, :]), ((1,), (1,)))
+        low_out[at, :] = sums + low[at, :]
+        copies.append(pltpu.make_async_copy(low_out.at[at], low_hbm.at[at], sem.at[n]))
+        copies[-1].start()
+    for copy in copies:
+        copy.wait()
 
 
 def shards(
@@ -391,10 +388,10 @@
 ):
     n_samp = lax.axis_size("samp")
     dma = pltpu.SemaphoreType.DMA
-    pair, give = call(
+    (give,) = call(
         table_kernel,
         [HBM] * 4,
-        [((2, ROWS, LANES), F32), ((SENT, LANES), F32)],
+        [((SENT, LANES), F32)],
         [pltpu.VMEM((20, 2, LANES), F32), pltpu.VMEM((20, 2, 512), F32)]
         + [pltpu.VMEM((16, 16), I32)] * 2
         + [dma((4,))],
@@ -407,28 +404,30 @@
         ((256, 256), BF16),
         ((256, 768), BF16),
         ((80, 768), F32),
+        ((2, ROWS, LANES), F32),
     ]
-    win, w, m, spins = call(
+    win, w, m, spins, pair = call(
         ready_kernel,
-        [HBM] * 6,
+        [HBM] * 8,
         made,
         [pltpu.VMEM((4, 2, 2, 4096), F32), pltpu.VMEM((16, 4096), F32), pltpu.VMEM(*made[0])]
         + [pltpu.VMEM((16, 768), I32), pltpu.VMEM((16, 768), F32), pltpu.VMEM((8, 768), F32)]
-        + [pltpu.VMEM(*x) for x in made[1:]]
+        + [pltpu.VMEM(*x) for x in made[1:4]]
         + [pltpu.VMEM((16, 16), I32)] * 2
-        + [dma((12,)), dma((4,))],
+        + [pltpu.VMEM((20, 2, LANES), F32), pltpu.VMEM((20, 2, 512), F32)]
+        + [pltpu.VMEM((ROWS, LANES), F32), dma((14,)), dma((5,))],
         flops=10 << 20,
         moved=8 << 20,
         out_place=HBM,
         room=ALL_VMEM,
-    )(radiated, stencil_index, stencil_weight, shift_angle, high_sources, high_operators)
+    )(radiated, stencil_index, stencil_weight, shift_angle, high_sources, high_operators, low_table, high_table)
     win, got = lax.optimization_barrier((win, got))
     win = lax.all_to_all(win, ("box", "samp"), 0, 0, tiled=True)
     tab = lax.all_gather(pair.at[1].set(got[:ROWS]), "rhs", tiled=True)
     part, rim = ((16, 8, LANES), F32), ((8, 8, LANES), F32)
     own, oth, rim_own, rim_oth = call(
         upper_kernel,
-        [VMEM] * 3 + [HBM] * 2,
+        [VMEM] * 5,
         [part, part, rim, rim],
         [
             pltpu.VMEM((2560, LANES), F32),
@@ -437,11 +436,9 @@
             pltpu.VMEM((256, LANES), F32),
             pltpu.VMEM((32, 8, LANES), F32),
             pltpu.VMEM((32, 8, LANES), F32),
-            pltpu.VMEM(*made[1]),
-            pltpu.VMEM((80, 256), F32),
             pltpu.VMEM((32, LANES), I32),
             pltpu.SMEM((32, LANES), I32),
-            dma((4,)),
+            dma,
         ],
         flops=200 << 20,
         moved=6 << 20,
@@ -476,9 +473,12 @@
         final_kernel,
         [VMEM] * 7,
         [((512, LANES), F32), ((16, 2, 2, 512), F32)],
-        [pltpu.VMEM((512, 768), BF16), pltpu.VMEM((512, 768), BF16)],
+        [pltpu.VMEM((512, LANES), F32), pltpu.VMEM((16, 2, 2, 512), F32)]
+        + [pltpu.VMEM((512, 768), BF16)] * 2
+        + [dma((5,))],
         flops=300 << 20,
         moved=4 << 20,
+        out_place=HBM,
     )(own, other, rim_a, rim_b, low.reshape(512, LANES), m, spins)
     return low_incoming.reshape(128, 2, 2, LANES), high_incoming
 

time: 71.3 us -> 70.9 us (level)
  Pallas kernels: 14.5 us -> 13.6 us
  transfers between devices with their start and end apart: 5 -> 5, of which waited for: 0 -> 1; matrix products, arithmetic and copies ran while one was open for 0% -> 0% of each run, Pallas kernels for 11% -> 11%
where the time goes in v2:
time: 70.9 us; the launch traced here: 70.5 us
  blocking collectives  28.3 us (40%)
  starting transfers between devices  27.6 us (39%)
  Pallas kernels  13.6 us (19%)
  between operations  0.81 us (1%)
    all_gather x1, blocking collectives, shards(): tab = lax.all_gather(pair.at[1].set(got[:ROWS]), 'rhs', tiled=True)  28.3 us
    all_to_all x1, starting transfers between devices, shards(): win = lax.all_to_all(win, ('box', 'samp'), 0, 0, tiled=True)  13.1 us
    ppermute x1, starting transfers between devices, shards(): lax.ppermute(rim_oth, both, [(i, flat(s, 1)) for i, s in down] + [(i, fla...  5.62 us
    pallas_call x1, Pallas kernels, shards(): call(lower_kernel, [VMEM] * 4, [((64, 8, LANES), F32)], [pltpu.VMEM((2560...  4.6 us
    ppermute x1, starting transfers between devices, shards(): other = lax.ppermute(oth, 'box', [(0, 1), (1, 0)])  3.5 us
    ppermute x1, starting transfers between devices, shards(): got = lax.ppermute(give, 'box', [(0, 1), (1, 0)])  3.4 us
    pallas_call x1, Pallas kernels, shards(): call(ready_kernel, [HBM] * 8, made, [pltpu.VMEM((4, 2, 2, 4096), F32), pl...  2.82 us
    pallas_call x1, Pallas kernels, shards(): call(upper_kernel, [VMEM] * 5, [part, part, rim, rim], [pltpu.VMEM((2560,...  2.48 us
  transfers between devices with their start and end apart: 5, of which 1 were waited for; matrix products, arithmetic and copies ran while one was open for 0% of the time, Pallas kernels for 11%

profile of v2, /device:TPU:64, one launch (start us, length us, event | category | flops | bytes accessed | tf_op | source)
XLA Modules:
  0.0 70.5 jit_solution(13052523975299370528)
XLA Ops:
  0.6 1.6 %shard_map.114 = f32[136,128]{1,0:T(8,128)} custom-call(f32[20,2,128]{2,1,0:T(2,128)} %low_hbm.3, f32[20,2,512]{2,1,0:T(2,128)} %high_hbm.3, s32[16,16]{1,0:T(8,128)} %sources_hbm.3, s32[16,16]{1,0:T(8,128)} %operators_hbm.3), custom_call_target="tpu_custom_call" | custom-call | bytes 1048576 | tf_op jit(solution)/shard_map/pallas_call | solution.py:391
  2.3 3.4 %collective-permute-start = (f32[136,128]{1,0:T(8,128)}, f32[136,128]{1,0:T(8,128)S(1)}, u32[]{:S(2)}, u32[]{:S(2)}) collective-permute-start(f32[136,128]{1,0:T(8,128)} %shard_map.114), channel_id=1, source_target_pairs={{0,8},{8,0},{1,9},{9,1},{2,10},{10,2},{3,11},{11,3},{4,12},{12,4},... | collective-permute-start | bytes 208904 | tf_op jit(solution)/shard_map/ppermute | solution.py:401
  5.7 2.8 %shard_map.113 = (f32[64,24,128]{2,1,0:T(8,128)}, bf16[256,256]{1,0:T(8,128)(2,1)}, bf16[256,768]{1,0:T(8,128)(2,1)}, f32[80,768]{1,0:T(8,128)}, f32[2,120,128]{2,1,0:T(8,128)}) custom-call(f32[4,2,2,4096]{3,2,1,0:T(2,128)} %rad_hbm.1, s32[16,16384]{1,0:T(8,128)} %index.1, f32[16,16384]{1,0:T(8,128)} %weight.1, f32[8,16384]{1,0:T(8,128)} %angle.1, ...), custom_call_target="tpu_custom_call" | custom-call | flops 10485760 | bytes 8388608 | tf_op jit(solution)/shard_map/pallas_call | solution.py:409
  8.5 0.2 collective-permute-done.got
  8.7 0.0 copy-start.5
  8.7 13.1 %all-to-all-start = ((f32[64,24,128]{2,1,0:T(8,128)}), f32[64,24,128]{2,1,0:T(8,128)S(1)}, u32[]{:S(2)}, u32[]{:S(2)}) async-start(f32[64,24,128]{2,1,0:T(8,128)} %get-tuple-element.30), calls=%async_computation | async-start | bytes 1572864 | tf_op jit(solution)/shard_map/all_to_all | solution.py:425
  21.8 0.0 copy-done.5
  21.8 0.0 copy-start
  21.9 0.0 copy-start.1
  21.9 28.3 %all_gather.3.tab = f32[16,120,128]{2,1,0:T(8,128)S(1)} all-gather(f32[2,120,128]{2,1,0:T(8,128)S(1)} %bitcast_dynamic-update-slice_fusion), channel_id=1, replica_groups=mesh['samp'=32,'box'=2,'rhs'=8] {'rhs'}, dimensions={0}, use_global_device_ids=true | all-gather | bytes 1105920 | tf_op jit(solution)/shard_map/all_gather | solution.py:426
  50.2 0.0 all-to-all-done.win
  50.2 0.0 copy-done
  50.2 0.0 copy-done.1
  50.2 0.0 copy-start.3
  50.2 2.5 %shard_map.115 = (f32[16,8,128]{2,1,0:T(8,128)S(1)}, f32[16,8,128]{2,1,0:T(8,128)S(1)}, f32[8,8,128]{2,1,0:T(8,128)S(1)}, f32[8,8,128]{2,1,0:T(8,128)S(1)}) custom-call(f32[16,120,128]{2,1,0:T(8,128)S(1)} %all_gather.3.tab, f32[136,128]{1,0:T(8,128)S(1)} %collective-permute-done.got, f32[64,24,128]{2,1,0:T(8,128)S(1)} %all-to-all-done.win, ...), custom_call_target="tpu_custom_call" | custom-call | flops 209715200 | bytes 6291456 | tf_op jit(solution)/shard_map/pallas_call | solution.py:428
  52.7 0.0 copy-start.2
  52.7 3.5 %collective-permute-start.1 = (f32[16,8,128]{2,1,0:T(8,128)S(1)}, f32[16,8,128]{2,1,0:T(8,128)S(1)}, u32[]{:S(2)}, u32[]{:S(2)}) collective-permute-start(f32[16,8,128]{2,1,0:T(8,128)S(1)} %get-tuple-element.34), channel_id=1, source_target_pairs={{0,8},{8,0},{1,9},{9,1},{2,10},{10,2},{3,11},{11,3},{4,12},{12,4},... | collective-permute-start | bytes 196616 | tf_op jit(solution)/shard_map/ppermute | solution.py:447
  56.2 1.9 %collective-permute-start.2 = (f32[8,8,128]{2,1,0:T(8,128)S(1)}, f32[8,8,128]{2,1,0:T(8,128)S(1)}, u32[]{:S(2)}, u32[]{:S(2)}) collective-permute-start(f32[8,8,128]{2,1,0:T(8,128)S(1)} %get-tuple-element.35), channel_id=1, source_target_pairs={{16,0},{32,16},{48,32},{64,48},{80,64},{96,80},{112,96},{128,112},... | collective-permute-start | bytes 98312 | tf_op jit(solution)/shard_map/ppermute | solution.py:451
  58.1 5.6 %collective-permute-start.3 = (f32[8,8,128]{2,1,0:T(8,128)S(1)}, f32[8,8,128]{2,1,0:T(8,128)S(1)}, u32[]{:S(2)}, u32[]{:S(2)}) collective-permute-start(f32[8,8,128]{2,1,0:T(8,128)S(1)} %get-tuple-element.36), channel_id=1, source_target_pairs={{16,8},{32,24},{48,40},{64,56},{80,72},{96,88},{112,104},{128,120}... | collective-permute-start | bytes 98312 | tf_op jit(solution)/shard_map/ppermute | solution.py:454
  63.8 0.0 copy-done.3
  63.8 0.0 copy-done.2
  63.8 0.0 copy-start.4
  63.8 4.6 %shard_map.116 = f32[64,8,128]{2,1,0:T(8,128)S(1)} custom-call(s32[16,128]{1,0:T(8,128)S(1)} %bitcast.7, s32[16,128]{1,0:T(8,128)S(1)} %bitcast.8, f32[64,24,128]{2,1,0:T(8,128)S(1)} %all-to-all-done.win, f32[16,120,128]{2,1,0:T(8,128)S(1)} %all_gather.3.tab), custom_call_target="tpu_custom_call" | custom-call | flops 20971520 | bytes 10485760 | tf_op jit(solution)/shard_map/pallas_call | solution.py:457
  68.4 0.0 collective-permute-done.2.rim_a
  68.4 0.0 collective-permute-done.3.rim_b
  68.4 0.0 collective-permute-done.1.got
  68.4 0.0 copy-done.4
  68.4 2.0 %shard_map.117 = (f32[512,128]{1,0:T(8,128)}, f32[16,2,2,512]{3,2,1,0:T(2,128)}) custom-call(f32[16,8,128]{2,1,0:T(8,128)S(1)} %get-tuple-element.33.own, f32[16,8,128]{2,1,0:T(8,128)S(1)} %collective-permute-done.1.got, f32[8,8,128]{2,1,0:T(8,128)S(1)} %collective-permute-done.2.rim_a, f32[8,8,128]{2,1,0:T(8,128)S(1)} %collective-permute-done.3.rim_b, ...), custom_call_target="tpu_custom_call" | custom-call | flops 314572800 | bytes 4194304 | tf_op jit(solution)/shard_map/pallas_call | solution.py:472
  (1 shorter events, 0.0 us)
Async XLA Ops:
  2.3 6.4 %collective-permute-start = (f32[136,128]{1,0:T(8,128)}, f32[136,128]{1,0:T(8,128)S(1)}, u32[]{:S(2)}, u32[]{:S(2)}) collective-permute-start(f32[136,128]{1,0:T(8,128)} %shard_map.114), channel_id=1, source_target_pairs={{0,8},{8,0},{1,9},{9,1},{2,10},{10,2},{3,11},{11,3},{4,12},{12,4},... | collective-permute-start | bytes 208904 | tf_op jit(solution)/shard_map/ppermute | solution.py:401
  8.7 13.1 %copy-start.5 = (f32[2,120,128]{2,1,0:T(8,128)S(1)}, f32[2,120,128]{2,1,0:T(8,128)}, u32[]{:S(2)}) copy-start(f32[2,120,128]{2,1,0:T(8,128)} %get-tuple-element.27) | copy-start | bytes 368644
  8.7 41.5 %all-to-all-start = ((f32[64,24,128]{2,1,0:T(8,128)}), f32[64,24,128]{2,1,0:T(8,128)S(1)}, u32[]{:S(2)}, u32[]{:S(2)}) async-start(f32[64,24,128]{2,1,0:T(8,128)} %get-tuple-element.30), calls=%async_computation | async-start | bytes 1572864 | tf_op jit(solution)/shard_map/all_to_all | solution.py:425
  21.8 28.3 %copy-start = (f32[80,768]{1,0:T(8,128)S(1)}, f32[80,768]{1,0:T(8,128)}, u32[]{:S(2)}) copy-start(f32[80,768]{1,0:T(8,128)} %get-tuple-element.32.spins) | copy-start | bytes 737284
  21.9 28.3 %copy-start.1 = (bf16[256,256]{1,0:T(8,128)(2,1)S(1)}, bf16[256,256]{1,0:T(8,128)(2,1)}, u32[]{:S(2)}) copy-start(bf16[256,256]{1,0:T(8,128)(2,1)} %get-tuple-element.31.w) | copy-start | bytes 393220
  50.2 13.6 %copy-start.3 = (s32[128,16]{0,1:T(8,128)S(1)}, s32[128,16]{0,1:T(8,128)}, u32[]{:S(2)}) copy-start(s32[128,16]{0,1:T(8,128)} %param.16) | copy-start | bytes 24580
  52.7 11.1 %copy-start.2 = (s32[128,16]{0,1:T(8,128)S(1)}, s32[128,16]{0,1:T(8,128)}, u32[]{:S(2)}) copy-start(s32[128,16]{0,1:T(8,128)} %param.15) | copy-start | bytes 24580
  52.7 15.7 %collective-permute-start.1 = (f32[16,8,128]{2,1,0:T(8,128)S(1)}, f32[16,8,128]{2,1,0:T(8,128)S(1)}, u32[]{:S(2)}, u32[]{:S(2)}) collective-permute-start(f32[16,8,128]{2,1,0:T(8,128)S(1)} %get-tuple-element.34), channel_id=1, source_target_pairs={{0,8},{8,0},{1,9},{9,1},{2,10},{10,2},{3,11},{11,3},{4,12},{12,4},... | collective-permute-start | bytes 196616 | tf_op jit(solution)/shard_map/ppermute | solution.py:447
  56.2 12.2 %collective-permute-start.2 = (f32[8,8,128]{2,1,0:T(8,128)S(1)}, f32[8,8,128]{2,1,0:T(8,128)S(1)}, u32[]{:S(2)}, u32[]{:S(2)}) collective-permute-start(f32[8,8,128]{2,1,0:T(8,128)S(1)} %get-tuple-element.35), channel_id=1, source_target_pairs={{16,0},{32,16},{48,32},{64,48},{80,64},{96,80},{112,96},{128,112},... | collective-permute-start | bytes 98312 | tf_op jit(solution)/shard_map/ppermute | solution.py:451
  58.1 10.3 %collective-permute-start.3 = (f32[8,8,128]{2,1,0:T(8,128)S(1)}, f32[8,8,128]{2,1,0:T(8,128)S(1)}, u32[]{:S(2)}, u32[]{:S(2)}) collective-permute-start(f32[8,8,128]{2,1,0:T(8,128)S(1)} %get-tuple-element.36), channel_id=1, source_target_pairs={{16,8},{32,24},{48,40},{64,56},{80,72},{96,88},{112,104},{128,120}... | collective-permute-start | bytes 98312 | tf_op jit(solution)/shard_map/ppermute | solution.py:454
  63.8 4.6 %copy-start.4 = (bf16[256,768]{1,0:T(8,128)(2,1)S(1)}, bf16[256,768]{1,0:T(8,128)(2,1)}, u32[]{:S(2)}) copy-start(bf16[256,768]{1,0:T(8,128)(2,1)} %get-tuple-element.37.m) | copy-start | bytes 1179652

commit v3 on v2

--- a/solution.py
+++ b/solution.py
@@ -224,7 +224,7 @@
         rows = jnp.concatenate([win[n * 8 + q, :16, :] for q in range(8)], 0)
         full[pl.ds(at, 128), :] = product3(halves(rows), (w[:LANES], w[LANES:]), ((1,), (0,)))
 
-    repeat(8, 4, interpolate)
+    repeat(8, 8, interpolate)
 
     def aggregate(u):
         at = pl.multiple_of(u * 32, 32)
@@ -240,7 +240,7 @@
             lay.append(total + pltpu.roll(total, 4, 0))
         pat[pl.ds(pl.multiple_of(u * 8, 8), 8), :] = jnp.where(upper, lay[0], lay[1])
 
-    repeat(32, 4, aggregate)
+    repeat(32, 8, aggregate)
     listed.wait()
 
     def translate(n):
@@ -255,7 +255,7 @@
                 acc2 += tim[op, :] * x
             same[u], cross[u] = acc, acc2
 
-    repeat(16, 2, translate)
+    repeat(16, 4, translate)
 
     def border(n):
         for whole, rim, shift in ((own, rim_own, 0), (oth, rim_oth, 16)):
@@ -310,7 +310,7 @@
                 acc[e % 2] += t8[op, :] * pat[src, :]
             full[32 * q + n] = acc[0] + acc[1]
 
-    repeat(32, 1, four)
+    repeat(32, 4, four)
 
     def fold(n):
         one, two = full[2 * n], full[2 * n + 1]
@@ -360,7 +360,7 @@
                 )
                 lh[pl.ds(at, 32), lanes], ll[pl.ds(at, 32), lanes] = halves(rows)
 
-    repeat(8, 2, pair)
+    repeat(8, 4, pair)
 
     copies = [pltpu.make_async_copy(high_out, high_hbm, sem.at[4])]
     copies[0].start()
@@ -423,7 +423,9 @@
     )(radiated, stencil_index, stencil_weight, shift_angle, high_sources, high_operators, low_table, high_table)
     win, got = lax.optimization_barrier((win, got))
     win = lax.all_to_all(win, ("box", "samp"), 0, 0, tiled=True)
-    tab = lax.all_gather(pair.at[1].set(got[:ROWS]), "rhs", tiled=True)
+    tab = lax.all_gather(
+        pair.at[1].set(got[:ROWS]).reshape(2 * ROWS, LANES), "rhs", tiled=True
+    ).reshape(16, ROWS, LANES)
     part, rim = ((16, 8, LANES), F32), ((8, 8, LANES), F32)
     own, oth, rim_own, rim_oth = call(
         upper_kernel,

time: 70.9 us -> 70.5 us (level)
  transfers between devices with their start and end apart: 5 -> 5, of which waited for: 1 -> 1; matrix products, arithmetic and copies ran while one was open for 0% -> 0% of each run, Pallas kernels for 11% -> 10%
where the time goes in v3:
time: 70.5 us; the launch traced here: 70.1 us
  blocking collectives  28.3 us (40%)
  starting transfers between devices  27.6 us (39%)
  Pallas kernels  13.2 us (19%)
  between operations  0.81 us (1%)
    all_gather x1, blocking collectives, shards(): lax.all_gather(pair.at[1].set(got[:ROWS]).reshape(2 * ROWS, LANES), 'rhs'...  28.3 us
    all_to_all x1, starting transfers between devices, shards(): win = lax.all_to_all(win, ('box', 'samp'), 0, 0, tiled=True)  13.1 us
    ppermute x1, starting transfers between devices, shards(): lax.ppermute(rim_oth, both, [(i, flat(s, 1)) for i, s in down] + [(i, fla...  5.62 us
    pallas_call x1, Pallas kernels, shards(): call(lower_kernel, [VMEM] * 4, [((64, 8, LANES), F32)], [pltpu.VMEM((2560...  4.42 us
    ppermute x1, starting transfers between devices, shards(): other = lax.ppermute(oth, 'box', [(0, 1), (1, 0)])  3.5 us
    ppermute x1, starting transfers between devices, shards(): got = lax.ppermute(give, 'box', [(0, 1), (1, 0)])  3.4 us
    pallas_call x1, Pallas kernels, shards(): call(ready_kernel, [HBM] * 8, made, [pltpu.VMEM((4, 2, 2, 4096), F32), pl...  2.82 us
    pallas_call x1, Pallas kernels, shards(): call(upper_kernel, [VMEM] * 5, [part, part, rim, rim], [pltpu.VMEM((2560,...  2.22 us
  transfers between devices with their start and end apart: 5, of which 1 were waited for; matrix products, arithmetic and copies ran while one was open for 0% of the time, Pallas kernels for 10%

profile of v3, /device:TPU:64, one launch (start us, length us, event | category | flops | bytes accessed | tf_op | source)
XLA Modules:
  0.0 70.1 jit_solution(2441310079286058064)
XLA Ops:
  0.6 1.6 %shard_map.114 = f32[136,128]{1,0:T(8,128)} custom-call(f32[20,2,128]{2,1,0:T(2,128)} %low_hbm.3, f32[20,2,512]{2,1,0:T(2,128)} %high_hbm.3, s32[16,16]{1,0:T(8,128)} %sources_hbm.3, s32[16,16]{1,0:T(8,128)} %operators_hbm.3), custom_call_target="tpu_custom_call" | custom-call | bytes 1048576 | tf_op jit(solution)/shard_map/pallas_call | solution.py:391
  2.3 3.4 %collective-permute-start = (f32[136,128]{1,0:T(8,128)}, f32[136,128]{1,0:T(8,128)S(1)}, u32[]{:S(2)}, u32[]{:S(2)}) collective-permute-start(f32[136,128]{1,0:T(8,128)} %shard_map.114), channel_id=1, source_target_pairs={{0,8},{8,0},{1,9},{9,1},{2,10},{10,2},{3,11},{11,3},{4,12},{12,4},... | collective-permute-start | bytes 208904 | tf_op jit(solution)/shard_map/ppermute | solution.py:401
  5.7 2.8 %shard_map.113 = (f32[64,24,128]{2,1,0:T(8,128)}, bf16[256,256]{1,0:T(8,128)(2,1)}, bf16[256,768]{1,0:T(8,128)(2,1)}, f32[80,768]{1,0:T(8,128)}, f32[2,120,128]{2,1,0:T(8,128)}) custom-call(f32[4,2,2,4096]{3,2,1,0:T(2,128)} %rad_hbm.1, s32[16,16384]{1,0:T(8,128)} %index.1, f32[16,16384]{1,0:T(8,128)} %weight.1, f32[8,16384]{1,0:T(8,128)} %angle.1, ...), custom_call_target="tpu_custom_call" | custom-call | flops 10485760 | bytes 8388608 | tf_op jit(solution)/shard_map/pallas_call | solution.py:409
  8.5 0.2 collective-permute-done.got
  8.7 0.0 copy-start.5
  8.7 13.1 %all-to-all-start = ((f32[64,24,128]{2,1,0:T(8,128)}), f32[64,24,128]{2,1,0:T(8,128)S(1)}, u32[]{:S(2)}, u32[]{:S(2)}) async-start(f32[64,24,128]{2,1,0:T(8,128)} %get-tuple-element.30), calls=%async_computation | async-start | bytes 1572864 | tf_op jit(solution)/shard_map/all_to_all | solution.py:425
  21.8 0.0 copy-done.5
  21.8 0.0 copy-start
  21.9 0.0 copy-start.1
  21.9 28.3 %all_gather.3 = f32[1920,128]{1,0:T(8,128)S(1)} all-gather(f32[240,128]{1,0:T(8,128)S(1)} %bitcast.13), channel_id=1, replica_groups=mesh['samp'=32,'box'=2,'rhs'=8] {'rhs'}, dimensions={0}, use_global_device_ids=true | all-gather | bytes 1105920 | tf_op jit(solution)/shard_map/all_gather | solution.py:426
  50.2 0.0 all-to-all-done.win
  50.2 0.0 copy-done
  50.2 0.0 copy-done.1
  50.2 0.0 copy-start.3
  50.2 2.2 %shard_map.115 = (f32[16,8,128]{2,1,0:T(8,128)S(1)}, f32[16,8,128]{2,1,0:T(8,128)S(1)}, f32[8,8,128]{2,1,0:T(8,128)S(1)}, f32[8,8,128]{2,1,0:T(8,128)S(1)}) custom-call(f32[16,120,128]{2,1,0:T(8,128)S(1)} %bitcast.8, f32[136,128]{1,0:T(8,128)S(1)} %collective-permute-done.got, f32[64,24,128]{2,1,0:T(8,128)S(1)} %all-to-all-done.win, ...), custom_call_target="tpu_custom_call" | custom-call | flops 209715200 | bytes 6291456 | tf_op jit(solution)/shard_map/pallas_call | solution.py:430
  52.4 0.0 copy-start.2
  52.4 3.5 %collective-permute-start.1 = (f32[16,8,128]{2,1,0:T(8,128)S(1)}, f32[16,8,128]{2,1,0:T(8,128)S(1)}, u32[]{:S(2)}, u32[]{:S(2)}) collective-permute-start(f32[16,8,128]{2,1,0:T(8,128)S(1)} %get-tuple-element.34), channel_id=1, source_target_pairs={{0,8},{8,0},{1,9},{9,1},{2,10},{10,2},{3,11},{11,3},{4,12},{12,4},... | collective-permute-start | bytes 196616 | tf_op jit(solution)/shard_map/ppermute | solution.py:449
  55.9 1.9 %collective-permute-start.2 = (f32[8,8,128]{2,1,0:T(8,128)S(1)}, f32[8,8,128]{2,1,0:T(8,128)S(1)}, u32[]{:S(2)}, u32[]{:S(2)}) collective-permute-start(f32[8,8,128]{2,1,0:T(8,128)S(1)} %get-tuple-element.35), channel_id=1, source_target_pairs={{16,0},{32,16},{48,32},{64,48},{80,64},{96,80},{112,96},{128,112},... | collective-permute-start | bytes 98312 | tf_op jit(solution)/shard_map/ppermute | solution.py:453
  57.9 5.6 %collective-permute-start.3 = (f32[8,8,128]{2,1,0:T(8,128)S(1)}, f32[8,8,128]{2,1,0:T(8,128)S(1)}, u32[]{:S(2)}, u32[]{:S(2)}) collective-permute-start(f32[8,8,128]{2,1,0:T(8,128)S(1)} %get-tuple-element.36), channel_id=1, source_target_pairs={{16,8},{32,24},{48,40},{64,56},{80,72},{96,88},{112,104},{128,120}... | collective-permute-start | bytes 98312 | tf_op jit(solution)/shard_map/ppermute | solution.py:456
  63.5 0.0 copy-done.3
  63.5 0.0 copy-done.2
  63.5 0.0 copy-start.4
  63.5 4.4 %shard_map.116 = f32[64,8,128]{2,1,0:T(8,128)S(1)} custom-call(s32[16,128]{1,0:T(8,128)S(1)} %bitcast.11, s32[16,128]{1,0:T(8,128)S(1)} %bitcast.12, f32[64,24,128]{2,1,0:T(8,128)S(1)} %all-to-all-done.win, f32[16,120,128]{2,1,0:T(8,128)S(1)} %bitcast.9), custom_call_target="tpu_custom_call" | custom-call | flops 20971520 | bytes 10485760 | tf_op jit(solution)/shard_map/pallas_call | solution.py:459
  68.0 0.0 collective-permute-done.2.rim_a
  68.0 0.0 collective-permute-done.3.rim_b
  68.0 0.0 collective-permute-done.1.got
  68.0 0.0 copy-done.4
  68.0 2.1 %shard_map.117 = (f32[512,128]{1,0:T(8,128)}, f32[16,2,2,512]{3,2,1,0:T(2,128)}) custom-call(f32[16,8,128]{2,1,0:T(8,128)S(1)} %get-tuple-element.33.own, f32[16,8,128]{2,1,0:T(8,128)S(1)} %collective-permute-done.1.got, f32[8,8,128]{2,1,0:T(8,128)S(1)} %collective-permute-done.2.rim_a, f32[8,8,128]{2,1,0:T(8,128)S(1)} %collective-permute-done.3.rim_b, ...), custom_call_target="tpu_custom_call" | custom-call | flops 314572800 | bytes 4194304 | tf_op jit(solution)/shard_map/pallas_call | solution.py:474
  (1 shorter events, 0.0 us)
Async XLA Ops:
  2.3 6.4 %collective-permute-start = (f32[136,128]{1,0:T(8,128)}, f32[136,128]{1,0:T(8,128)S(1)}, u32[]{:S(2)}, u32[]{:S(2)}) collective-permute-start(f32[136,128]{1,0:T(8,128)} %shard_map.114), channel_id=1, source_target_pairs={{0,8},{8,0},{1,9},{9,1},{2,10},{10,2},{3,11},{11,3},{4,12},{12,4},... | collective-permute-start | bytes 208904 | tf_op jit(solution)/shard_map/ppermute | solution.py:401
  8.7 13.1 %copy-start.5 = (f32[2,120,128]{2,1,0:T(8,128)S(1)}, f32[2,120,128]{2,1,0:T(8,128)}, u32[]{:S(2)}) copy-start(f32[2,120,128]{2,1,0:T(8,128)} %get-tuple-element.27) | copy-start | bytes 368644
  8.7 41.5 %all-to-all-start = ((f32[64,24,128]{2,1,0:T(8,128)}), f32[64,24,128]{2,1,0:T(8,128)S(1)}, u32[]{:S(2)}, u32[]{:S(2)}) async-start(f32[64,24,128]{2,1,0:T(8,128)} %get-tuple-element.30), calls=%async_computation | async-start | bytes 1572864 | tf_op jit(solution)/shard_map/all_to_all | solution.py:425
  21.8 28.3 %copy-start = (f32[80,768]{1,0:T(8,128)S(1)}, f32[80,768]{1,0:T(8,128)}, u32[]{:S(2)}) copy-start(f32[80,768]{1,0:T(8,128)} %get-tuple-element.32.spins) | copy-start | bytes 737284
  21.9 28.3 %copy-start.1 = (bf16[256,256]{1,0:T(8,128)(2,1)S(1)}, bf16[256,256]{1,0:T(8,128)(2,1)}, u32[]{:S(2)}) copy-start(bf16[256,256]{1,0:T(8,128)(2,1)} %get-tuple-element.31.w) | copy-start | bytes 393220
  50.2 13.3 %copy-start.3 = (s32[128,16]{0,1:T(8,128)S(1)}, s32[128,16]{0,1:T(8,128)}, u32[]{:S(2)}) copy-start(s32[128,16]{0,1:T(8,128)} %param.16) | copy-start | bytes 24580
  52.4 11.1 %copy-start.2 = (s32[128,16]{0,1:T(8,128)S(1)}, s32[128,16]{0,1:T(8,128)}, u32[]{:S(2)}) copy-start(s32[128,16]{0,1:T(8,128)} %param.15) | copy-start | bytes 24580
  52.4 15.6 %collective-permute-start.1 = (f32[16,8,128]{2,1,0:T(8,128)S(1)}, f32[16,8,128]{2,1,0:T(8,128)S(1)}, u32[]{:S(2)}, u32[]{:S(2)}) collective-permute-start(f32[16,8,128]{2,1,0:T(8,128)S(1)} %get-tuple-element.34), channel_id=1, source_target_pairs={{0,8},{8,0},{1,9},{9,1},{2,10},{10,2},{3,11},{11,3},{4,12},{12,4},... | collective-permute-start | bytes 196616 | tf_op jit(solution)/shard_map/ppermute | solution.py:449
  55.9 12.0 %collective-permute-start.2 = (f32[8,8,128]{2,1,0:T(8,128)S(1)}, f32[8,8,128]{2,1,0:T(8,128)S(1)}, u32[]{:S(2)}, u32[]{:S(2)}) collective-permute-start(f32[8,8,128]{2,1,0:T(8,128)S(1)} %get-tuple-element.35), channel_id=1, source_target_pairs={{16,0},{32,16},{48,32},{64,48},{80,64},{96,80},{112,96},{128,112},... | collective-permute-start | bytes 98312 | tf_op jit(solution)/shard_map/ppermute | solution.py:453
  57.9 10.1 %collective-permute-start.3 = (f32[8,8,128]{2,1,0:T(8,128)S(1)}, f32[8,8,128]{2,1,0:T(8,128)S(1)}, u32[]{:S(2)}, u32[]{:S(2)}) collective-permute-start(f32[8,8,128]{2,1,0:T(8,128)S(1)} %get-tuple-element.36), channel_id=1, source_target_pairs={{16,8},{32,24},{48,40},{64,56},{80,72},{96,88},{112,104},{128,120}... | collective-permute-start | bytes 98312 | tf_op jit(solution)/shard_map/ppermute | solution.py:456
  63.5 4.5 %copy-start.4 = (bf16[256,768]{1,0:T(8,128)(2,1)S(1)}, bf16[256,768]{1,0:T(8,128)(2,1)}, u32[]{:S(2)}) copy-start(bf16[256,768]{1,0:T(8,128)(2,1)} %get-tuple-element.37.m) | copy-start | bytes 1179652

commit v4 on v3

--- a/solution.py
+++ b/solution.py
@@ -217,7 +217,7 @@
             tre[pl.ds(at, 8), :] = jnp.where(upper, across(four, 0), across(four, 2))
             tim[pl.ds(at, 8), :] = jnp.where(upper, across(four, 1), across(four, 3)) * flip
 
-    repeat(16, 2, device)
+    repeat(16, 4, device)
 
     def interpolate(n):
         at = pl.multiple_of(n * 128, 128)
@@ -240,7 +240,7 @@
             lay.append(total + pltpu.roll(total, 4, 0))
         pat[pl.ds(pl.multiple_of(u * 8, 8), 8), :] = jnp.where(upper, lay[0], lay[1])
 
-    repeat(32, 8, aggregate)
+    repeat(32, 16, aggregate)
     listed.wait()
 
     def translate(n):
@@ -255,7 +255,7 @@
                 acc2 += tim[op, :] * x
             same[u], cross[u] = acc, acc2
 
-    repeat(16, 4, translate)
+    repeat(16, 8, translate)
 
     def border(n):
         for whole, rim, shift in ((own, rim_own, 0), (oth, rim_oth, 16)):
@@ -288,7 +288,7 @@
             at = pl.multiple_of(first + 8 * i, 8)
             t8[pl.ds(at, 8), :] = jnp.where(upper, across(two, 0), across(two, 1)) * flip
 
-    repeat(16, 2, device)
+    repeat(16, 4, device)
     def spread_out(n):
         extra = win[n, 16:24, :]
         for v, x in enumerate((extra, pltpu.roll(extra, 64, 1))):
@@ -310,7 +310,7 @@
                 acc[e % 2] += t8[op, :] * pat[src, :]
             full[32 * q + n] = acc[0] + acc[1]
 
-    repeat(32, 4, four)
+    repeat(32, 8, four)
 
     def fold(n):
         one, two = full[2 * n], full[2 * n + 1]
@@ -360,7 +360,7 @@
                 )
                 lh[pl.ds(at, 32), lanes], ll[pl.ds(at, 32), lanes] = halves(rows)
 
-    repeat(8, 4, pair)
+    repeat(8, 8, pair)
 
     copies = [pltpu.make_async_copy(high_out, high_hbm, sem.at[4])]
     copies[0].start()

time: 70.5 us -> 69.9 us (level)
  no operation moved by 1% of the time
where the time goes in v4:
time: 69.9 us; the launch traced here: 69.6 us
  blocking collectives  28.3 us (40%)
  starting transfers between devices  27.6 us (39%)
  Pallas kernels  12.6 us (18%)
  between operations  0.81 us (1%)
    all_gather x1, blocking collectives, shards(): lax.all_gather(pair.at[1].set(got[:ROWS]).reshape(2 * ROWS, LANES), 'rhs'...  28.3 us
    all_to_all x1, starting transfers between devices, shards(): win = lax.all_to_all(win, ('box', 'samp'), 0, 0, tiled=True)  13.1 us
    ppermute x1, starting transfers between devices, shards(): lax.ppermute(rim_oth, both, [(i, flat(s, 1)) for i, s in down] + [(i, fla...  5.63 us
    pallas_call x1, Pallas kernels, shards(): call(lower_kernel, [VMEM] * 4, [((64, 8, LANES), F32)], [pltpu.VMEM((2560...  4.36 us
    ppermute x1, starting transfers between devices, shards(): other = lax.ppermute(oth, 'box', [(0, 1), (1, 0)])  3.5 us
    ppermute x1, starting transfers between devices, shards(): got = lax.ppermute(give, 'box', [(0, 1), (1, 0)])  3.4 us
    pallas_call x1, Pallas kernels, shards(): call(ready_kernel, [HBM] * 8, made, [pltpu.VMEM((4, 2, 2, 4096), F32), pl...  2.82 us
    pallas_call x1, Pallas kernels, shards(): call(upper_kernel, [VMEM] * 5, [part, part, rim, rim], [pltpu.VMEM((2560,...  2.15 us
  transfers between devices with their start and end apart: 5, of which 1 were waited for; matrix products, arithmetic and copies ran while one was open for 0% of the time, Pallas kernels for 10%

profile of v4, /device:TPU:64, one launch (start us, length us, event | category | flops | bytes accessed | tf_op | source)
XLA Modules:
  0.0 69.6 jit_solution(701842146655823723)
XLA Ops:
  0.6 1.6 %shard_map.114 = f32[136,128]{1,0:T(8,128)} custom-call(f32[20,2,128]{2,1,0:T(2,128)} %low_hbm.3, f32[20,2,512]{2,1,0:T(2,128)} %high_hbm.3, s32[16,16]{1,0:T(8,128)} %sources_hbm.3, s32[16,16]{1,0:T(8,128)} %operators_hbm.3), custom_call_target="tpu_custom_call" | custom-call | bytes 1048576 | tf_op jit(solution)/shard_map/pallas_call | solution.py:391
  2.3 3.4 %collective-permute-start = (f32[136,128]{1,0:T(8,128)}, f32[136,128]{1,0:T(8,128)S(1)}, u32[]{:S(2)}, u32[]{:S(2)}) collective-permute-start(f32[136,128]{1,0:T(8,128)} %shard_map.114), channel_id=1, source_target_pairs={{0,8},{8,0},{1,9},{9,1},{2,10},{10,2},{3,11},{11,3},{4,12},{12,4},... | collective-permute-start | bytes 208904 | tf_op jit(solution)/shard_map/ppermute | solution.py:401
  5.7 2.8 %shard_map.113 = (f32[64,24,128]{2,1,0:T(8,128)}, bf16[256,256]{1,0:T(8,128)(2,1)}, bf16[256,768]{1,0:T(8,128)(2,1)}, f32[80,768]{1,0:T(8,128)}, f32[2,120,128]{2,1,0:T(8,128)}) custom-call(f32[4,2,2,4096]{3,2,1,0:T(2,128)} %rad_hbm.1, s32[16,16384]{1,0:T(8,128)} %index.1, f32[16,16384]{1,0:T(8,128)} %weight.1, f32[8,16384]{1,0:T(8,128)} %angle.1, ...), custom_call_target="tpu_custom_call" | custom-call | flops 10485760 | bytes 8388608 | tf_op jit(solution)/shard_map/pallas_call | solution.py:409
  8.5 0.2 collective-permute-done.got
  8.7 0.0 copy-start.5
  8.7 13.1 %all-to-all-start = ((f32[64,24,128]{2,1,0:T(8,128)}), f32[64,24,128]{2,1,0:T(8,128)S(1)}, u32[]{:S(2)}, u32[]{:S(2)}) async-start(f32[64,24,128]{2,1,0:T(8,128)} %get-tuple-element.30), calls=%async_computation | async-start | bytes 1572864 | tf_op jit(solution)/shard_map/all_to_all | solution.py:425
  21.8 0.0 copy-done.5
  21.8 0.0 copy-start
  21.9 0.0 copy-start.1
  21.9 28.3 %all_gather.3 = f32[1920,128]{1,0:T(8,128)S(1)} all-gather(f32[240,128]{1,0:T(8,128)S(1)} %bitcast.13), channel_id=1, replica_groups=mesh['samp'=32,'box'=2,'rhs'=8] {'rhs'}, dimensions={0}, use_global_device_ids=true | all-gather | bytes 1105920 | tf_op jit(solution)/shard_map/all_gather | solution.py:426
  50.2 0.0 all-to-all-done.win
  50.2 0.0 copy-done
  50.2 0.0 copy-done.1
  50.2 0.0 copy-start.3
  50.2 2.2 %shard_map.115 = (f32[16,8,128]{2,1,0:T(8,128)S(1)}, f32[16,8,128]{2,1,0:T(8,128)S(1)}, f32[8,8,128]{2,1,0:T(8,128)S(1)}, f32[8,8,128]{2,1,0:T(8,128)S(1)}) custom-call(f32[16,120,128]{2,1,0:T(8,128)S(1)} %bitcast.8, f32[136,128]{1,0:T(8,128)S(1)} %collective-permute-done.got, f32[64,24,128]{2,1,0:T(8,128)S(1)} %all-to-all-done.win, ...), custom_call_target="tpu_custom_call" | custom-call | flops 209715200 | bytes 6291456 | tf_op jit(solution)/shard_map/pallas_call | solution.py:430
  52.4 0.0 copy-start.2
  52.4 3.5 %collective-permute-start.1 = (f32[16,8,128]{2,1,0:T(8,128)S(1)}, f32[16,8,128]{2,1,0:T(8,128)S(1)}, u32[]{:S(2)}, u32[]{:S(2)}) collective-permute-start(f32[16,8,128]{2,1,0:T(8,128)S(1)} %get-tuple-element.34), channel_id=1, source_target_pairs={{0,8},{8,0},{1,9},{9,1},{2,10},{10,2},{3,11},{11,3},{4,12},{12,4},... | collective-permute-start | bytes 196616 | tf_op jit(solution)/shard_map/ppermute | solution.py:449
  55.9 1.9 %collective-permute-start.2 = (f32[8,8,128]{2,1,0:T(8,128)S(1)}, f32[8,8,128]{2,1,0:T(8,128)S(1)}, u32[]{:S(2)}, u32[]{:S(2)}) collective-permute-start(f32[8,8,128]{2,1,0:T(8,128)S(1)} %get-tuple-element.35), channel_id=1, source_target_pairs={{16,0},{32,16},{48,32},{64,48},{80,64},{96,80},{112,96},{128,112},... | collective-permute-start | bytes 98312 | tf_op jit(solution)/shard_map/ppermute | solution.py:453
  57.8 5.6 %collective-permute-start.3 = (f32[8,8,128]{2,1,0:T(8,128)S(1)}, f32[8,8,128]{2,1,0:T(8,128)S(1)}, u32[]{:S(2)}, u32[]{:S(2)}) collective-permute-start(f32[8,8,128]{2,1,0:T(8,128)S(1)} %get-tuple-element.36), channel_id=1, source_target_pairs={{16,8},{32,24},{48,40},{64,56},{80,72},{96,88},{112,104},{128,120}... | collective-permute-start | bytes 98312 | tf_op jit(solution)/shard_map/ppermute | solution.py:456
  63.4 0.0 copy-done.3
  63.4 0.0 copy-done.2
  63.5 0.0 copy-start.4
  63.5 4.4 %shard_map.116 = f32[64,8,128]{2,1,0:T(8,128)S(1)} custom-call(s32[16,128]{1,0:T(8,128)S(1)} %bitcast.11, s32[16,128]{1,0:T(8,128)S(1)} %bitcast.12, f32[64,24,128]{2,1,0:T(8,128)S(1)} %all-to-all-done.win, f32[16,120,128]{2,1,0:T(8,128)S(1)} %bitcast.9), custom_call_target="tpu_custom_call" | custom-call | flops 20971520 | bytes 10485760 | tf_op jit(solution)/shard_map/pallas_call | solution.py:459
  67.8 0.0 collective-permute-done.2.rim_a
  67.8 0.0 collective-permute-done.3.rim_b
  67.9 0.0 collective-permute-done.1.got
  67.9 0.0 copy-done.4
  67.9 1.7 %shard_map.117 = (f32[512,128]{1,0:T(8,128)}, f32[16,2,2,512]{3,2,1,0:T(2,128)}) custom-call(f32[16,8,128]{2,1,0:T(8,128)S(1)} %get-tuple-element.33.own, f32[16,8,128]{2,1,0:T(8,128)S(1)} %collective-permute-done.1.got, f32[8,8,128]{2,1,0:T(8,128)S(1)} %collective-permute-done.2.rim_a, f32[8,8,128]{2,1,0:T(8,128)S(1)} %collective-permute-done.3.rim_b, ...), custom_call_target="tpu_custom_call" | custom-call | flops 314572800 | bytes 4194304 | tf_op jit(solution)/shard_map/pallas_call | solution.py:474
  (1 shorter events, 0.0 us)
Async XLA Ops:
  2.3 6.4 %collective-permute-start = (f32[136,128]{1,0:T(8,128)}, f32[136,128]{1,0:T(8,128)S(1)}, u32[]{:S(2)}, u32[]{:S(2)}) collective-permute-start(f32[136,128]{1,0:T(8,128)} %shard_map.114), channel_id=1, source_target_pairs={{0,8},{8,0},{1,9},{9,1},{2,10},{10,2},{3,11},{11,3},{4,12},{12,4},... | collective-permute-start | bytes 208904 | tf_op jit(solution)/shard_map/ppermute | solution.py:401
  8.7 13.1 %copy-start.5 = (f32[2,120,128]{2,1,0:T(8,128)S(1)}, f32[2,120,128]{2,1,0:T(8,128)}, u32[]{:S(2)}) copy-start(f32[2,120,128]{2,1,0:T(8,128)} %get-tuple-element.27) | copy-start | bytes 368644
  8.7 41.5 %all-to-all-start = ((f32[64,24,128]{2,1,0:T(8,128)}), f32[64,24,128]{2,1,0:T(8,128)S(1)}, u32[]{:S(2)}, u32[]{:S(2)}) async-start(f32[64,24,128]{2,1,0:T(8,128)} %get-tuple-element.30), calls=%async_computation | async-start | bytes 1572864 | tf_op jit(solution)/shard_map/all_to_all | solution.py:425
  21.8 28.3 %copy-start = (f32[80,768]{1,0:T(8,128)S(1)}, f32[80,768]{1,0:T(8,128)}, u32[]{:S(2)}) copy-start(f32[80,768]{1,0:T(8,128)} %get-tuple-element.32.spins) | copy-start | bytes 737284
  21.9 28.3 %copy-start.1 = (bf16[256,256]{1,0:T(8,128)(2,1)S(1)}, bf16[256,256]{1,0:T(8,128)(2,1)}, u32[]{:S(2)}) copy-start(bf16[256,256]{1,0:T(8,128)(2,1)} %get-tuple-element.31.w) | copy-start | bytes 393220
  50.2 13.3 %copy-start.3 = (s32[128,16]{0,1:T(8,128)S(1)}, s32[128,16]{0,1:T(8,128)}, u32[]{:S(2)}) copy-start(s32[128,16]{0,1:T(8,128)} %param.16) | copy-start | bytes 24580
  52.4 11.1 %copy-start.2 = (s32[128,16]{0,1:T(8,128)S(1)}, s32[128,16]{0,1:T(8,128)}, u32[]{:S(2)}) copy-start(s32[128,16]{0,1:T(8,128)} %param.15) | copy-start | bytes 24580
  52.4 15.5 %collective-permute-start.1 = (f32[16,8,128]{2,1,0:T(8,128)S(1)}, f32[16,8,128]{2,1,0:T(8,128)S(1)}, u32[]{:S(2)}, u32[]{:S(2)}) collective-permute-start(f32[16,8,128]{2,1,0:T(8,128)S(1)} %get-tuple-element.34), channel_id=1, source_target_pairs={{0,8},{8,0},{1,9},{9,1},{2,10},{10,2},{3,11},{11,3},{4,12},{12,4},... | collective-permute-start | bytes 196616 | tf_op jit(solution)/shard_map/ppermute | solution.py:449
  55.9 12.0 %collective-permute-start.2 = (f32[8,8,128]{2,1,0:T(8,128)S(1)}, f32[8,8,128]{2,1,0:T(8,128)S(1)}, u32[]{:S(2)}, u32[]{:S(2)}) collective-permute-start(f32[8,8,128]{2,1,0:T(8,128)S(1)} %get-tuple-element.35), channel_id=1, source_target_pairs={{16,0},{32,16},{48,32},{64,48},{80,64},{96,80},{112,96},{128,112},... | collective-permute-start | bytes 98312 | tf_op jit(solution)/shard_map/ppermute | solution.py:453
  57.8 10.0 %collective-permute-start.3 = (f32[8,8,128]{2,1,0:T(8,128)S(1)}, f32[8,8,128]{2,1,0:T(8,128)S(1)}, u32[]{:S(2)}, u32[]{:S(2)}) collective-permute-start(f32[8,8,128]{2,1,0:T(8,128)S(1)} %get-tuple-element.36), channel_id=1, source_target_pairs={{16,8},{32,24},{48,40},{64,56},{80,72},{96,88},{112,104},{128,120}... | collective-permute-start | bytes 98312 | tf_op jit(solution)/shard_map/ppermute | solution.py:456
  63.5 4.4 %copy-start.4 = (bf16[256,768]{1,0:T(8,128)(2,1)S(1)}, bf16[256,768]{1,0:T(8,128)(2,1)}, u32[]{:S(2)}) copy-start(bf16[256,768]{1,0:T(8,128)(2,1)} %get-tuple-element.37.m) | copy-start | bytes 1179652
